TPU v7x, 128 devices: a whole 4x4x4 slice. The times are simulated.
128 devices in a mesh: rep: 4 (over z), con: 32 (over y, x, core).
Axes of the slice: x: 4, y: 4, z: 4, core: 2. Of those that a mesh axis runs over, the one named last changes fastest.
Arguments:
- amplitudes: bfloat16 [4, 8, 100, 16000], P(None, None, None, ('rep', 'con')), may hold values from -8 to 8
- block_table: int32 [4, 8], replicated, may hold values 0 or 1
- intermediate: bfloat16 [4, 16000, 16000], P(None, 'rep', 'con'), may hold values from -0.046875 to 0.046875
- slab_energy: float32 [8], replicated, may hold values from -1 to -0.3
- slab_irrep: int32 [8], replicated, may hold values from 0 to 7
- occ_energy: float32 [8, 20], replicated, may hold values from -1 to -0.3
- virt_energy: float32 [8, 100], replicated, may hold values from 0.1 to 1.5
Outputs:
- update: bfloat16 [4, 8, 100, 16000], P(None, 'rep', None, 'con')
All inputs are finite; a program needn't handle non-finite values.
Results may differ from a plain program's by a relative error of at most 0.001.
Values may be sent and summed in bfloat16 or wider, within the bound.
No kernel may reach another device: no remote copies, remote signals or barrier semaphores. Data moves between devices by JAX's collectives and lax.ppermute only.
A program may use at most 192 MiB of HBM per device.

v0:
```python
import jax
import jax.numpy as jnp
from jax import lax
from jax.sharding import PartitionSpec as P


def make_accumulate(inter_block, table_block, rep_offset, pair_width, irreps, shard_cols):
    count = shard_cols.shape[3]
    columns = rep_offset + jnp.arange(count, dtype=jnp.int32)
    col_irrep = columns // pair_width
    hits = col_irrep[:, None] == jnp.arange(irreps, dtype=jnp.int32)[None, :]
    keep = jnp.sum(jnp.where(hits[None], table_block[:, None, :], 0), axis=2).astype(jnp.bfloat16)
    masked = shard_cols * keep[:, None, None, :]
    return jnp.einsum("hiap,hpq->hiaq", masked, inter_block, preferred_element_type=jnp.float32)


def denominators(cycle_shape, slab_energy, slab_irrep, occ_energy, virt_energy):
    block_count, rows_here, virt_width, col_count = cycle_shape
    occ_width = occ_energy.shape[1]
    irreps = occ_energy.shape[0]
    row_start = lax.axis_index("rep") * rows_here
    energy_i = lax.dynamic_slice_in_dim(slab_energy, row_start, rows_here)
    labels = lax.dynamic_slice_in_dim(slab_irrep, row_start, rows_here)
    block_ids = jnp.arange(block_count, dtype=jnp.int32)
    a_irrep = jnp.bitwise_xor(labels[None, :], block_ids[:, None])
    hits_a = a_irrep[:, :, None] == jnp.arange(irreps, dtype=jnp.int32)[None, None, :]
    energy_a = jnp.sum(jnp.where(hits_a[..., None], virt_energy[None, None], 0.0), axis=2)
    columns = lax.axis_index("con") * col_count + jnp.arange(col_count, dtype=jnp.int32)
    pair_index = columns // virt_width
    virt_index = columns % virt_width
    pair_irrep = pair_index // occ_width
    occ_flat = occ_energy.reshape(-1)
    hits_j = pair_index[:, None] == jnp.arange(occ_flat.shape[0], dtype=jnp.int32)[None, :]
    energy_j = jnp.sum(jnp.where(hits_j, occ_flat[None, :], 0.0), axis=1)
    virt_flat = virt_energy.reshape(-1)
    b_index = (
        jnp.bitwise_xor(pair_irrep[None, :], block_ids[:, None]) * virt_width + virt_index[None, :]
    )
    hits_b = b_index[..., None] == jnp.arange(virt_flat.shape[0], dtype=jnp.int32)[None, None, :]
    energy_b = jnp.sum(jnp.where(hits_b, virt_flat[None, None, :], 0.0), axis=2)
    return (
        energy_i[None, :, None, None]
        + energy_j[None, None, None, :]
        - energy_a[:, :, :, None]
        - energy_b[:, None, None, :]
    )


def shards(amplitudes, block_table, intermediate, slab_energy, slab_irrep, occ_energy, virt_energy):
    quarter = intermediate.shape[1]
    irreps = occ_energy.shape[0]
    pair_width = occ_energy.shape[1] * virt_energy.shape[1]
    rep_offset = lax.axis_index("rep") * quarter
    folded = make_accumulate(
        intermediate,
        block_table,
        rep_offset,
        pair_width,
        irreps,
        lax.all_gather(amplitudes, "con", axis=3, tiled=True),
    )
    cycle = lax.psum_scatter(folded, "rep", scatter_dimension=1, tiled=True)
    denominator = denominators(cycle.shape, slab_energy, slab_irrep, occ_energy, virt_energy)
    return (cycle / denominator).astype(jnp.bfloat16)


def solution(mesh):
    placed = (P(None, None, None, ("rep", "con")), P(), P(None, "rep", "con"), P(), P(), P(), P())
    return jax.shard_map(
        shards, mesh=mesh, in_specs=placed, out_specs=P(None, "rep", None, "con"), check_vma=False
    )
```

profile of v0, /device:TPU:1, one launch (start us, length us, event | category | flops | bytes accessed | tf_op | source)
XLA Modules:
  0.0 334.1 jit_solution(8465090216562276935)
XLA Ops:
  6.5 2.9 copy.14
  9.4 0.0 all-reduce.3.cloned.1.call-start
  9.5 0.9 select_reduce_fusion.1
  10.5 0.5 copy.15
  11.0 113.9 %all-gather.2.cloned.1.call-done = bf16[4,8,100,4000]{2,1,0,3:T(8,128)(2,1)} async-done(((bf16[4,8,100,125]{2,1,0,3:T(8,128)(2,1)}), bf16[4,8,100,4000]{2,1,0,3:T(8,128)(2,1)}) %all-gather.2.cloned.1.call-update) | async-done | bytes 25600016 | tf_op jit(solution)/shard_map/all_gather | solution.py:60
  124.9 22.4 %broadcast_multiply_fusion = bf16[4,8,100,4000]{2,1,0,3:T(8,128)(2,1)} fusion(bf16[4,8,100,4000]{2,1,0,3:T(8,128)(2,1)} %all-gather.2.cloned.1.call-done, bf16[4,4000]{0,1:T(8,128)(2,1)S(1)} %copy.15), kind=kLoop, calls=%fused_computation.3 | loop fusion | flops 12800000 | bytes 51232000 | tf_op jit(solution)/shard_map/mul | solution.py:13
  147.3 35.7 %fusion = f32[4,8,100,500]{3,2,1,0:T(8,128)} fusion(bf16[4,8,100,4000]{2,1,0,3:T(8,128)(2,1)} %broadcast_multiply_fusion, bf16[4,4000,500]{2,1,0:T(8,128)(2,1)} %param.9), kind=kOutput, calls=%fused_computation | convolution fusion | flops 12800000000 | bytes 48000000 | tf_op jit(solution)/shard_map/hiap,hpq->hiaq/dot_general | solution.py:14
  183.0 9.9 %copy.17 = f32[4,8,100,500]{3,0,2,1:T(4,128)} copy(f32[4,8,100,500]{3,2,1,0:T(8,128)} %fusion) | data formatting | bytes 12800000 | tf_op jit(solution)/shard_map/hiap,hpq->hiaq/dot_general | solution.py:14
  192.9 0.0 all-reduce.3.cloned.1.call-update
  193.0 0.6 copy-done
  193.6 0.1 broadcast_in_dim.99
  193.7 0.1 dynamic_slice.7
  193.8 0.1 iota_compare_fusion.3
  193.9 0.1 select_reduce_fusion.3
  194.0 0.1 copy.18
  194.1 0.1 broadcast_in_dim.93
  194.2 0.1 dynamic_slice.6
  194.3 0.6 dynamic-slice
  195.6 0.1 select_reduce_fusion.2
  195.7 0.1 broadcast_add_fusion
  195.8 0.9 select_reduce_fusion
  196.7 126.8 %all-reduce.3.cloned.1.call-done = f32[4,8,100,500]{3,0,2,1:T(4,128)} async-done(((f32[4,8,100,500]{3,0,2,1:T(4,128)}), f32[4,8,100,500]{3,0,2,1:T(4,128)}) %all-reduce.3.cloned.1.call-update) | async-done | bytes 6400016
  323.5 2.0 fusion.3
  325.5 1.7 copy.19
  (18 shorter events, 0.1 us)
Async XLA Ops:
  6.5 118.4 %all-gather.2.cloned.1.call-start = ((), (), s32[]{:S(2)}) async-start(), calls=%async_computation | async-start | bytes 33792000 | tf_op jit(solution)/shard_map/all_gather | solution.py:60
  9.4 314.0 %all-reduce.3.cloned.1.call-start = ((), (), s32[]{:S(2)}) async-start(), calls=%async_computation.1 | async-start | bytes 13107200
  192.9 0.7 copy-start
  192.9 0.8 copy-start.2
  192.9 1.2 copy-start.1
  192.9 1.3 copy-start.3
  192.9 1.3 copy-start.4
Sparse Core Ops, SparseCore 0:
  9.6 115.2 all-gather.1
  193.1 130.3 all-reduce.2
where the time goes:
time: 334 us
  waiting for transfers between devices  241 us (72%)
  matrix products  35.7 us (11%)
  other arithmetic  26.7 us (8%)
  local copies, waits for them, and re-layouts  16.7 us (5%)
  between operations  14.2 us (4%)
    unnamed x3, waiting for transfers between devices  127 us
    all_gather x1, waiting for transfers between devices, shards(): lax.all_gather(amplitudes, 'con', axis=3, tiled=True)  114 us
    dot_general x1, matrix products, make_accumulate(): jnp.einsum('hiap,hpq->hiaq', masked, inter_block, preferred_element_type=...  35.7 us
    mul x1, other arithmetic, make_accumulate(): masked = shard_cols * keep[:, None, None, :]  22.4 us
    dot_general x1, local copies, waits for them, and re-layouts, make_accumulate(): jnp.einsum('hiap,hpq->hiaq', masked, inter_block, preferred_element_type=...  9.89 us
  transfers between devices with their start and end apart: 2, of which 2 were waited for; matrix products, arithmetic and copies ran while one was open for 1% of the time, Pallas kernels for 0%

commit v1 on v0

v1 whole, which is shorter than its diff:
```python
import functools

import jax
import jax.numpy as jnp
from jax import lax
from jax.experimental import pallas as pl
from jax.experimental.pallas import tpu as pltpu
from jax.sharding import PartitionSpec as P

SIDE = 4
SHARD = 128
COLS = 512
OFFSETS = (0, -1, 1, 2)
PARTS = (((0, 200),), ((0, 104), (104, 200)))
STEPS = 64.0
LEAST = 2.0**-125
TOP = 32766.0
PARAMS = pltpu.CompilerParams(vmem_limit_bytes=24 * 1024 * 1024)


def ring_pairs(stage, hop):
    pairs = []
    for y in range(SIDE):
        for x in range(SIDE):
            for core in range(2):
                if (core + stage) % 2 == 0:
                    to_x, to_y = (x + hop) % SIDE, y
                else:
                    to_x, to_y = x, (y + hop) % SIDE
                pairs.append(((y * SIDE + x) * 2 + core, (to_y * SIDE + to_x) * 2 + core))
    return pairs


def ring(value, stage, hop):
    return lax.ppermute(value, "con", ring_pairs(stage, hop))


def swap_cores(value):
    return lax.ppermute(value, "con", [(i, i ^ 1) for i in range(2 * SIDE * SIDE)])


def to_replica(value, hop):
    return lax.ppermute(value, "rep", [(i, (i + hop) % SIDE) for i in range(SIDE)])


def code_rows(acc, table, own, codes):
    _, _, rows, cols = acc.shape
    lane = lax.broadcasted_iota(jnp.int32, (rows, cols), 1)
    for side in range(2):
        own[side] = acc[side, table[17]]
        for hop, code in enumerate(codes):
            value = acc[side, table[18 + hop]]
            most = jnp.maximum(jnp.max(jnp.abs(value), axis=1, keepdims=True), LEAST)
            level = jnp.ceil(jnp.log2(most) * STEPS)
            scaled = value * jnp.exp2(level * (-1.0 / STEPS)) * TOP
            code[side] = jnp.where(lane == cols - 1, level, jnp.round(scaled)).astype(jnp.int32).astype(jnp.int16)


def product_kernel(
    h, chip_cols, table, t0, t1, t2, t3, w_own, w_other, own, code1, code2, code3, t_buf, w_buf, acc, t_sem, w_sem
):
    _, reps, rows, cols = acc.shape
    depth, width = w_own.shape[1:]
    chips = t_buf.shape[0]
    block = table[16] * 2 + h
    edges = [-(-chip_cols * SIDE * g // 16) * 16 for g in range(SIDE)] + [depth]
    w_copies = []
    for g in range(SIDE):
        span = pl.ds(edges[g], edges[g + 1] - edges[g])
        for side, w in enumerate((w_own, w_other)):
            w_copies.append(pltpu.make_async_copy(w.at[block, span], w_buf.at[side, span], w_sem.at[g, side]))
    for copy in w_copies[:2]:
        copy.start()
    for j, t_ref in enumerate((t0, t1, t2, t3)):
        for i in range(SIDE):
            chip = table[j * SIDE + i]
            pltpu.make_async_copy(t_ref.at[i], t_buf.at[chip], t_sem.at[chip]).start()
    for copy in w_copies[2:]:
        copy.start()
    tail = w_buf.shape[1] - depth
    for side in range(2):
        w_buf[side, depth:, :] = jnp.zeros((tail, width), w_buf.dtype)
    for g in range(SIDE):
        group = range(g * SIDE, (g + 1) * SIDE)
        for copy in w_copies[2 * g : 2 * g + 2]:
            copy.wait()
        for chip in group:
            pltpu.make_async_copy(t0.at[0], t_buf.at[chip], t_sem.at[chip]).wait()
        left = jnp.concatenate([t_buf[chip] for chip in group], axis=1)
        for side in range(2):
            windows = [w_buf[side, chip * chip_cols : chip * chip_cols + 2 * SHARD, :] for chip in group]
            part = jnp.dot(left, jnp.concatenate(windows, axis=0), preferred_element_type=jnp.float32)
            part = part.reshape(reps, rows, width)
            if g == 0:
                acc[side, :, :, width:] = jnp.zeros((reps, rows, cols - width), jnp.float32)
                acc[side, :, :, :width] = part
            else:
                acc[side, :, :, :width] += part
    code_rows(acc, table, own, (code1, code2, code3))


def multiply(table, h, chip_cols, t_parts, w_own, w_other):
    count, rows4, lanes = t_parts[0].shape
    rows = rows4 // SIDE
    depth, width = w_own.shape[1:]
    chips = SIDE * count
    code_shape = (2, rows, COLS)
    whole = pl.BlockSpec(memory_space=pl.ANY)
    return pl.pallas_call(
        functools.partial(product_kernel, h, chip_cols),
        grid_spec=pltpu.PrefetchScalarGridSpec(
            num_scalar_prefetch=1,
            grid=(1,),
            in_specs=[whole] * 6,
            out_specs=[pl.BlockSpec(code_shape, lambda k, tab: (0, 0, 0))] * 4,
            scratch_shapes=[
                pltpu.VMEM((chips, rows4, lanes), jnp.bfloat16),
                pltpu.VMEM((2, depth + 16, width), jnp.bfloat16),
                pltpu.VMEM((2, SIDE, rows, COLS), jnp.float32),
                pltpu.SemaphoreType.DMA((chips,)),
                pltpu.SemaphoreType.DMA((SIDE, 2)),
            ],
        ),
        out_shape=[jax.ShapeDtypeStruct(code_shape, jnp.float32)] + [jax.ShapeDtypeStruct(code_shape, jnp.int16)] * 3,
        compiler_params=PARAMS,
        cost_estimate=pl.CostEstimate(
            flops=2 * rows4 * depth * 2 * width, bytes_accessed=2 * depth * width * 2 * 3, transcendentals=0
        ),
    )(table, *t_parts, w_own, w_other)


def finish_kernel(own, code1, code2, code3, rows_e, cols_e, out_own, out_other):
    cols = own.shape[2]
    for side, out in enumerate((out_own, out_other)):
        total = own[side]
        for code in (code1, code2, code3):
            whole = code[side].astype(jnp.int32).astype(jnp.float32)
            level = whole[:, cols - 1 :]
            total = total + whole * (jnp.exp2(level * (1.0 / STEPS)) * (1.0 / TOP))
        denominator = rows_e[:, 0:1] + cols_e[side, 0:1, :] - rows_e[:, 1:2] - cols_e[side, 1:2, :]
        out[...] = (total / denominator).astype(jnp.bfloat16)[:, : out.shape[1]]


def finish(own, codes, rows_e, cols_e, width):
    rows = own.shape[1]
    return pl.pallas_call(
        finish_kernel,
        out_shape=[jax.ShapeDtypeStruct((rows, width), jnp.bfloat16)] * 2,
        compiler_params=PARAMS,
        cost_estimate=pl.CostEstimate(flops=10 * own.size, bytes_accessed=2_000_000, transcendentals=0),
    )(own, *codes, rows_e, cols_e)


def row_energies(my_h, slab_energy, slab_irrep, virt_energy):
    irreps = virt_energy.shape[0]
    here = slab_energy.shape[0] // SIDE
    start = lax.axis_index("rep") * here
    energy_i = lax.dynamic_slice_in_dim(slab_energy, start, here)
    labels = lax.dynamic_slice_in_dim(slab_irrep, start, here)
    a_irrep = jnp.bitwise_xor(labels[None, :], my_h[:, None])
    hits = a_irrep[:, :, None] == jnp.arange(irreps, dtype=jnp.int32)
    energy_a = jnp.sum(jnp.where(hits[..., None], virt_energy[None, None], 0.0), axis=2)
    energy_i = jnp.broadcast_to(energy_i[None, :, None], energy_a.shape)
    return jnp.stack([energy_i, energy_a], axis=3).reshape(my_h.shape[0], -1, 2)


def col_energies(my_h, con, width, occ_energy, virt_energy):
    irreps, occ_width = occ_energy.shape
    virt_width = virt_energy.shape[1]
    columns = con * width + jnp.arange(COLS, dtype=jnp.int32)
    pair_index = columns // virt_width
    virt_index = columns % virt_width
    pair_irrep = pair_index // occ_width
    hits_j = pair_index[:, None] == jnp.arange(irreps * occ_width, dtype=jnp.int32)
    energy_j = jnp.sum(jnp.where(hits_j, occ_energy.reshape(-1), 0.0), axis=1)
    b_index = jnp.bitwise_xor(pair_irrep[None, :], my_h[:, None]) * virt_width + virt_index[None, :]
    hits_b = b_index[..., None] == jnp.arange(irreps * virt_width, dtype=jnp.int32)
    energy_b = jnp.sum(jnp.where(hits_b, virt_energy.reshape(-1), 0.0), axis=2)
    inside = jnp.arange(COLS) < width
    energy_j = jnp.broadcast_to(jnp.where(inside, energy_j, -1.0)[None], energy_b.shape)
    return jnp.stack([energy_j, energy_b], axis=1)


def shards(amplitudes, block_table, intermediate, slab_energy, slab_irrep, occ_energy, virt_energy):
    blocks, slab, virt, shard = amplitudes.shape
    width = intermediate.shape[2]
    rows = slab * virt
    per_rep = rows // SIDE
    mine = blocks // 2
    rep, con = lax.axis_index("rep"), lax.axis_index("con")
    core, chip = con % 2, con // 2
    y, x = chip // SIDE, chip % SIDE
    pair_width = occ_energy.shape[1] * virt_energy.shape[1]

    group = (rep * 2 * SIDE * SIDE + con) * shard // pair_width
    keep = lax.dynamic_index_in_dim(block_table, group, axis=1, keepdims=False).astype(jnp.bfloat16)
    masked = amplitudes * keep[:, None, None, None]
    masked = masked.reshape(blocks, rows, shard)
    kept = lax.dynamic_slice_in_dim(masked, core * mine, mine)
    given = lax.dynamic_slice_in_dim(masked, (1 - core) * mine, mine)
    got = swap_cores(given)
    t = jnp.where(core == 0, jnp.concatenate([kept, got], axis=2), jnp.concatenate([got, kept], axis=2))
    t = jnp.pad(t, ((0, 0), (0, 0), (0, 2 * SHARD - 2 * shard)))
    w_other = swap_cores(intermediate)

    near = (jnp.array(OFFSETS, jnp.int32)[None, :], jnp.array(OFFSETS, jnp.int32)[:, None])
    x_chip = jnp.where(core == 0, near[0], near[1])
    y_chip = jnp.where(core == 0, near[1], near[0])
    chips = jnp.mod(y + y_chip, SIDE) * SIDE + jnp.mod(x + x_chip, SIDE)
    table = jnp.concatenate(
        [chips.reshape(-1), core[None], jnp.mod(rep + jnp.arange(SIDE, dtype=jnp.int32), SIDE)]
    ).astype(jnp.int32)

    my_h = core * mine + jnp.arange(mine, dtype=jnp.int32)
    rows_e = row_energies(my_h, slab_energy, slab_irrep, virt_energy)
    cols_e = jnp.stack(
        [col_energies(my_h, c, width, occ_energy, virt_energy) for c in (con, jnp.bitwise_xor(con, 1))], axis=1
    )

    kept, got = [], []
    for h in range(mine):
        before, after = ring(t[h], 0, 1), ring(t[h], 0, -1)
        hop = 1 if h == 0 else -1
        far = ring(before if h == 0 else after, 0, hop)
        row = jnp.stack([t[h], before, after, far]).reshape(SIDE, SIDE, per_rep, 2 * SHARD)
        for first, last in PARTS[h]:
            here = row[:, :, first:last].reshape(SIDE, -1, 2 * SHARD)
            row_before, row_after = ring(here, 1, 1), ring(here, 1, -1)
            row_far = ring(row_before if h == 0 else row_after, 1, hop)
            t_parts = (here, row_before, row_after, row_far)
            own, *codes = multiply(table, h, 2 * shard, t_parts, intermediate, w_other)
            codes = [to_replica(code, hops + 1) for hops, code in enumerate(codes)]
            out_own, out_other = finish(own, codes, rows_e[h, first:last], cols_e[h], width)
            kept.append(out_own)
            got.append(swap_cores(out_other))

    kept, got = jnp.concatenate(kept), jnp.concatenate(got)
    out = jnp.where(core == 0, jnp.concatenate([kept, got]), jnp.concatenate([got, kept]))
    return out.reshape(blocks, slab // SIDE, virt, width)


def solution(mesh):
    placed = (P(None, None, None, ("rep", "con")), P(), P(None, "rep", "con"), P(), P(), P(), P())
    return jax.shard_map(
        shards, mesh=mesh, in_specs=placed, out_specs=P(None, "rep", None, "con"), check_vma=False
    )
```

time: 334 us -> 173 us (0.52)
  waiting for transfers between devices: 241 us -> 75.6 us
  starting transfers between devices: 0.04 us -> 42.5 us
  matrix products: 35.7 us -> 0 us
  Pallas kernels: 0 us -> 30.6 us
  other arithmetic: 26.7 us -> 8.89 us
  between operations: 14.2 us -> 0.46 us
    unnamed x3 -> x0, waiting for transfers between devices: 127 us -> none
    all_gather x1 -> x0, waiting for transfers between devices: 114 us -> none  [shards(): lax.all_gather(amplitudes, 'con', axis=3, tiled=True)]
    ppermute x0 -> x29, waiting for transfers between devices: none -> 75.6 us  [the longest x15 48.9 us: ring(): return lax.ppermute(value, 'con', ring_pairs(stage, hop))]
    ppermute x0 -> x29, starting transfers between devices: none -> 42.5 us  [the longest x15 18.2 us: ring(): return lax.ppermute(value, 'con', ring_pairs(stage, hop))]
    dot_general x1 -> x0, matrix products: 35.7 us -> none  [make_accumulate(): jnp.einsum('hiap,hpq->hiaq', masked, inter_block, preferred_element_type=...]
    pallas_call x0 -> x6, Pallas kernels: none -> 30.6 us  [the longest x3 29.4 us: multiply(): pl.pallas_call(functools.partial(product_kernel, h, chip_cols), grid_spec...]
    mul x1, other arithmetic: 22.4 us -> 1.27 us  [shards(): masked = amplitudes * keep[:, None, None, None]]
    dot_general x1 -> x0, local copies, waits for them, and re-layouts: 9.89 us -> none  [make_accumulate(): jnp.einsum('hiap,hpq->hiaq', masked, inter_block, preferred_element_type=...]
  transfers between devices with their start and end apart: 2 -> 29, of which waited for: 2 -> 11; matrix products, arithmetic and copies ran while one was open for 1% -> 8% of each run, Pallas kernels for 0% -> 18%
where the time goes in v1:
time: 173 us
  waiting for transfers between devices  75.6 us (44%)
  starting transfers between devices  42.5 us (25%)
  Pallas kernels  30.6 us (18%)
  local copies, waits for them, and re-layouts  14.7 us (8%)
  other arithmetic  8.89 us (5%)
    ppermute x15, waiting for transfers between devices, ring(): return lax.ppermute(value, 'con', ring_pairs(stage, hop))  48.9 us
    pallas_call x3, Pallas kernels, multiply(): pl.pallas_call(functools.partial(product_kernel, h, chip_cols), grid_spec...  29.4 us
    ppermute x5, waiting for transfers between devices, swap_cores(): lax.ppermute(value, 'con', [(i, i ^ 1) for i in range(2 * SIDE * SIDE)])  23 us
    ppermute x15, starting transfers between devices, ring(): return lax.ppermute(value, 'con', ring_pairs(stage, hop))  18.2 us
    ppermute x9, starting transfers between devices, to_replica(): lax.ppermute(value, 'rep', [(i, (i + hop) % SIDE) for i in range(SIDE)])  13.9 us
    ppermute x5, starting transfers between devices, swap_cores(): lax.ppermute(value, 'con', [(i, i ^ 1) for i in range(2 * SIDE * SIDE)])  10.4 us
    unnamed x33, local copies, waits for them, and re-layouts  8.66 us
    ppermute x9, waiting for transfers between devices, to_replica(): lax.ppermute(value, 'rep', [(i, (i + hop) % SIDE) for i in range(SIDE)])  3.7 us
  transfers between devices with their start and end apart: 29, of which 11 were waited for; matrix products, arithmetic and copies ran while one was open for 8% of the time, Pallas kernels for 18%

profile of v1, /device:TPU:1, one launch (start us, length us, event | category | flops | bytes accessed | tf_op | source)
XLA Modules:
  0.0 172.6 jit_solution(7706646478852898280)
XLA Ops:
  4.2 22.1 %collective-permute-done = bf16[2,800,125]{2,1,0:T(8,128)(2,1)S(1)} collective-permute-done((bf16[2,800,125]{2,1,0:T(8,128)(2,1)S(1)}, bf16[2,800,125]{2,1,0:T(8,128)(2,1)S(1)}, u32[]{:S(2)}, u32[]{:S(2)}) %collective-permute-start) | collective-permute-done | bytes 400032 | tf_op jit(solution)/shard_map/ppermute | solution.py:39
  30.8 5.6 %collective-permute-done.1 = bf16[800,256]{1,0:T(8,128)(2,1)S(1)} collective-permute-done((bf16[800,256]{1,0:T(8,128)(2,1)S(1)}, bf16[800,256]{1,0:T(8,128)(2,1)S(1)}, u32[]{:S(2)}, u32[]{:S(2)}) %collective-permute-start.1) | collective-permute-done | bytes 409632 | tf_op jit(solution)/shard_map/ppermute | solution.py:35
  36.4 8.3 %collective-permute-done.3 = bf16[800,256]{1,0:T(8,128)(2,1)S(1)} collective-permute-done((bf16[800,256]{1,0:T(8,128)(2,1)S(1)}, bf16[800,256]{1,0:T(8,128)(2,1)S(1)}, u32[]{:S(2)}, u32[]{:S(2)}) %collective-permute-start.3) | collective-permute-done | bytes 409632 | tf_op jit(solution)/shard_map/ppermute | solution.py:35
  48.6 4.9 %collective-permute-done.12 = bf16[800,256]{1,0:T(8,128)(2,1)} collective-permute-done((bf16[800,256]{1,0:T(8,128)(2,1)}, bf16[800,256]{1,0:T(8,128)(2,1)}, u32[]{:S(2)}, u32[]{:S(2)}) %collective-permute-start.12) | collective-permute-done | bytes 409632 | tf_op jit(solution)/shard_map/ppermute | solution.py:35
  53.4 1.8 %collective-permute-start.13 = (bf16[800,256]{1,0:T(8,128)(2,1)}, bf16[800,256]{1,0:T(8,128)(2,1)}, u32[]{:S(2)}, u32[]{:S(2)}) collective-permute-start(bf16[800,256]{1,0:T(8,128)(2,1)} %collective-permute-done.12), channel_id=1, source_target_pairs={{0,6},{1,25},{2,0},{3,27},{4,2},{5,29},{6,4},{7,31},{8,14},{9,1},{... | collective-permute-start | bytes 1228808 | tf_op jit(solution)/shard_map/ppermute | solution.py:35
  55.4 2.0 %collective-permute-start.5 = (bf16[4,800,256]{2,1,0:T(8,128)(2,1)S(1)}, bf16[4,800,256]{2,1,0:T(8,128)(2,1)}, u32[]{:S(2)}, u32[]{:S(2)}) collective-permute-start(bf16[4,800,256]{2,1,0:T(8,128)(2,1)S(1)} %pad_maximum_fusion.t0), channel_id=1, source_target_pairs={{0,24},{1,7},{2,26},{3,1},{4,28},{5,3},{6,30},{7,5},{8,0},{9,15},{... | collective-permute-start | bytes 4915208 | tf_op jit(solution)/shard_map/ppermute | solution.py:35
  57.3 13.6 %collective-permute-done.4.t1 = bf16[4,800,256]{2,1,0:T(8,128)(2,1)S(1)} collective-permute-done((bf16[4,800,256]{2,1,0:T(8,128)(2,1)S(1)}, bf16[4,800,256]{2,1,0:T(8,128)(2,1)S(1)}, u32[]{:S(2)}, u32[]{:S(2)}) %collective-permute-start.4) | collective-permute-done | bytes 1638432 | tf_op jit(solution)/shard_map/ppermute | solution.py:35
  71.2 2.6 %pad_maximum_fusion.2 = bf16[4,4,96,256]{3,2,1,0:T(8,128)(2,1)} fusion(bf16[1,4,200,256]{3,2,1,0:T(8,128)(2,1)} %bitcast.13, bf16[1,4,200,256]{3,2,1,0:T(8,128)(2,1)} %bitcast.12, bf16[1,4,200,256]{3,2,1,0:T(8,128)(2,1)} %bitcast.11, bf16[1,4,200,256]{3,2,1,0:T(8,128)(2,1)} %bitcast.29), kind=kLoop, calls=%fused_computation.8 | loop fusion | flops 3145728 | bytes 2424832 | tf_op jit(solution)/shard_map/slice | solution.py:227
  73.8 2.3 %collective-permute-start.21 = (bf16[4,384,256]{2,1,0:T(8,128)(2,1)}, bf16[4,384,256]{2,1,0:T(8,128)(2,1)}, u32[]{:S(2)}, u32[]{:S(2)}) collective-permute-start(bf16[4,384,256]{2,1,0:T(8,128)(2,1)} %bitcast.17.t0), channel_id=1, source_target_pairs={{0,24},{1,7},{2,26},{3,1},{4,28},{5,3},{6,30},{7,5},{8,0},{9,15},{... | collective-permute-start | bytes 2359304 | tf_op jit(solution)/shard_map/ppermute | solution.py:35
  80.1 8.5 %collective-permute-done.21.t2 = bf16[4,384,256]{2,1,0:T(8,128)(2,1)} collective-permute-done((bf16[4,384,256]{2,1,0:T(8,128)(2,1)}, bf16[4,384,256]{2,1,0:T(8,128)(2,1)}, u32[]{:S(2)}, u32[]{:S(2)}) %collective-permute-start.21) | collective-permute-done | bytes 786464 | tf_op jit(solution)/shard_map/ppermute | solution.py:35
  89.8 7.9 %collective-permute-done.15.t2 = bf16[4,416,256]{2,1,0:T(8,128)(2,1)} collective-permute-done((bf16[4,416,256]{2,1,0:T(8,128)(2,1)}, bf16[4,416,256]{2,1,0:T(8,128)(2,1)}, u32[]{:S(2)}, u32[]{:S(2)}) %collective-permute-start.15) | collective-permute-done | bytes 852000 | tf_op jit(solution)/shard_map/ppermute | solution.py:35
  97.8 3.1 %collective-permute-start.22 = (bf16[4,384,256]{2,1,0:T(8,128)(2,1)}, bf16[4,384,256]{2,1,0:T(8,128)(2,1)}, u32[]{:S(2)}, u32[]{:S(2)}) collective-permute-start(bf16[4,384,256]{2,1,0:T(8,128)(2,1)} %collective-permute-done.21.t2), channel_id=1, source_target_pairs={{0,24},{1,7},{2,26},{3,1},{4,28},{5,3},{6,30},{7,5},{8,0},{9,15},{... | collective-permute-start | bytes 2359304 | tf_op jit(solution)/shard_map/ppermute | solution.py:35
  101.1 2.7 %collective-permute-start.16 = (bf16[4,416,256]{2,1,0:T(8,128)(2,1)}, bf16[4,416,256]{2,1,0:T(8,128)(2,1)}, u32[]{:S(2)}, u32[]{:S(2)}) collective-permute-start(bf16[4,416,256]{2,1,0:T(8,128)(2,1)} %collective-permute-done.15.t2), channel_id=1, source_target_pairs={{0,24},{1,7},{2,26},{3,1},{4,28},{5,3},{6,30},{7,5},{8,0},{9,15},{... | collective-permute-start | bytes 2555912 | tf_op jit(solution)/shard_map/ppermute | solution.py:35
  103.7 5.7 %copy-done = bf16[4,4000,500]{2,1,0:T(8,128)(2,1)S(1)} copy-done((bf16[4,4000,500]{2,1,0:T(8,128)(2,1)S(1)}, bf16[4,4000,500]{2,1,0:T(8,128)(2,1)}, u32[]{:S(2)}) %copy-start) | copy-done | bytes 16000024
  112.2 13.6 %shard_map.91 = (f32[2,200,512]{2,1,0:T(8,128)S(1)}, s16[2,200,512]{2,1,0:T(8,128)(2,1)}, s16[2,200,512]{2,1,0:T(8,128)(2,1)S(1)}, s16[2,200,512]{2,1,0:T(8,128)(2,1)S(1)}) custom-call(s32[21]{0:T(128)S(1)} %pad_add_fusion.table, bf16[4,800,256]{2,1,0:T(8,128)(2,1)S(1)} %copy-done.3, bf16[4,800,256]{2,1,0:T(8,128)(2,1)S(1)} %copy-done.5, ...), custom_call_target="tpu_custom_call" | custom-call | flops 6400000000 | bytes 24000000 | tf_op jit(solution)/shard_map/pallas_call | solution.py:109
  125.8 3.8 %collective-permute-start.10 = (s16[2,200,512]{2,1,0:T(8,128)(2,1)S(1)}, s16[2,200,512]{2,1,0:T(8,128)(2,1)S(1)}, u32[]{:S(2)}, u32[]{:S(2)}) collective-permute-start(s16[2,200,512]{2,1,0:T(8,128)(2,1)S(1)} %get-tuple-element.26), channel_id=1, source_target_pairs={{0,96},{32,0},{64,32},{96,64},{1,97},{33,1},{65,33},{97,65},{2,98}... | collective-permute-start | bytes 1228808 | tf_op jit(solution)/shard_map/ppermute | solution.py:43
  130.9 7.7 %shard_map.95 = (f32[2,96,512]{2,1,0:T(8,128)S(1)}, s16[2,96,512]{2,1,0:T(8,128)(2,1)S(1)}, s16[2,96,512]{2,1,0:T(8,128)(2,1)S(1)}, s16[2,96,512]{2,1,0:T(8,128)(2,1)S(1)}) custom-call(s32[21]{0:T(128)S(1)} %pad_add_fusion.table, bf16[4,384,256]{2,1,0:T(8,128)(2,1)} %bitcast.17.t0, bf16[4,384,256]{2,1,0:T(8,128)(2,1)} %collective-permute-done.20.t1, ...), custom_call_target="tpu_custom_call" | custom-call | flops 3072000000 | bytes 24000000 | tf_op jit(solution)/shard_map/pallas_call | solution.py:109
  138.7 2.0 %collective-permute-start.23 = (s16[2,96,512]{2,1,0:T(8,128)(2,1)S(1)}, s16[2,96,512]{2,1,0:T(8,128)(2,1)S(1)}, u32[]{:S(2)}, u32[]{:S(2)}) collective-permute-start(s16[2,96,512]{2,1,0:T(8,128)(2,1)S(1)} %get-tuple-element.34), channel_id=1, source_target_pairs={{0,32},{32,64},{64,96},{96,0},{1,33},{33,65},{65,97},{97,1},{2,34}... | collective-permute-start | bytes 589832 | tf_op jit(solution)/shard_map/ppermute | solution.py:43
  141.3 8.1 %shard_map.93 = (f32[2,104,512]{2,1,0:T(8,128)S(1)}, s16[2,104,512]{2,1,0:T(8,128)(2,1)S(1)}, s16[2,104,512]{2,1,0:T(8,128)(2,1)S(1)}, s16[2,104,512]{2,1,0:T(8,128)(2,1)S(1)}) custom-call(s32[21]{0:T(128)S(1)} %pad_add_fusion.table, bf16[4,416,256]{2,1,0:T(8,128)(2,1)} %bitcast.14.t0, bf16[4,416,256]{2,1,0:T(8,128)(2,1)} %collective-permute-done.14.t1, ...), custom_call_target="tpu_custom_call" | custom-call | flops 3328000000 | bytes 24000000 | tf_op jit(solution)/shard_map/pallas_call | solution.py:109
  150.2 3.6 %collective-permute-start.25 = (s16[2,96,512]{2,1,0:T(8,128)(2,1)S(1)}, s16[2,96,512]{2,1,0:T(8,128)(2,1)S(1)}, u32[]{:S(2)}, u32[]{:S(2)}) collective-permute-start(s16[2,96,512]{2,1,0:T(8,128)(2,1)S(1)} %get-tuple-element.36), channel_id=1, source_target_pairs={{0,96},{32,0},{64,32},{96,64},{1,97},{33,1},{65,33},{97,65},{2,98}... | collective-permute-start | bytes 589832 | tf_op jit(solution)/shard_map/ppermute | solution.py:43
  157.1 3.7 %collective-permute-start.26 = (bf16[200,500]{1,0:T(8,128)(2,1)S(1)}, bf16[200,500]{1,0:T(8,128)(2,1)S(1)}, u32[]{:S(2)}, u32[]{:S(2)}) collective-permute-start(bf16[200,500]{1,0:T(8,128)(2,1)S(1)} %get-tuple-element.38), channel_id=1, source_target_pairs={{0,1},{1,0},{2,3},{3,2},{4,5},{5,4},{6,7},{7,6},{8,9},{9,8},{10,11... | collective-permute-start | bytes 600008 | tf_op jit(solution)/shard_map/ppermute | solution.py:39
  161.4 4.0 %collective-permute-start.28 = (bf16[96,500]{1,0:T(8,128)(2,1)S(1)}, bf16[96,500]{1,0:T(8,128)(2,1)S(1)}, u32[]{:S(2)}, u32[]{:S(2)}) collective-permute-start(bf16[96,500]{1,0:T(8,128)(2,1)S(1)} %get-tuple-element.40), channel_id=1, source_target_pairs={{0,1},{1,0},{2,3},{3,2},{4,5},{5,4},{6,7},{7,6},{8,9},{9,8},{10,11... | collective-permute-start | bytes 288008 | tf_op jit(solution)/shard_map/ppermute | solution.py:39
  165.4 2.7 %collective-permute-done.17.code1 = s16[2,104,512]{2,1,0:T(8,128)(2,1)S(1)} collective-permute-done((s16[2,104,512]{2,1,0:T(8,128)(2,1)S(1)}, s16[2,104,512]{2,1,0:T(8,128)(2,1)S(1)}, u32[]{:S(2)}, u32[]{:S(2)}) %collective-permute-start.17) | collective-permute-done | bytes 213024 | tf_op jit(solution)/shard_map/ppermute | solution.py:43
  171.1 1.5 copy.26
  (128 shorter events, 30.5 us)
Async XLA Ops:
  0.0 103.7 %collective-permute-start.7 = (bf16[4,4000,500]{2,1,0:T(8,128)(2,1)}, bf16[4,4000,500]{2,1,0:T(8,128)(2,1)}, u32[]{:S(2)}, u32[]{:S(2)}) collective-permute-start(bf16[4,4000,500]{2,1,0:T(8,128)(2,1)} %w_own.5), channel_id=1, source_target_pairs={{0,1},{1,0},{2,3},{3,2},{4,5},{5,4},{6,7},{7,6},{8,9},{9,8},{10,11... | collective-permute-start | bytes 48000008 | tf_op jit(solution)/shard_map/ppermute | solution.py:39
  4.1 22.2 %collective-permute-start = (bf16[2,800,125]{2,1,0:T(8,128)(2,1)S(1)}, bf16[2,800,125]{2,1,0:T(8,128)(2,1)S(1)}, u32[]{:S(2)}, u32[]{:S(2)}) collective-permute-start(bf16[2,800,125]{2,1,0:T(8,128)(2,1)S(1)} %get-tuple-element.50), channel_id=1, source_target_pairs={{0,1},{1,0},{2,3},{3,2},{4,5},{5,4},{6,7},{7,6},{8,9},{9,8},{10,11... | collective-permute-start | bytes 1200008 | tf_op jit(solution)/shard_map/ppermute | solution.py:39
  45.0 25.9 %collective-permute-start.4 = (bf16[4,800,256]{2,1,0:T(8,128)(2,1)S(1)}, bf16[4,800,256]{2,1,0:T(8,128)(2,1)S(1)}, u32[]{:S(2)}, u32[]{:S(2)}) collective-permute-start(bf16[4,800,256]{2,1,0:T(8,128)(2,1)S(1)} %pad_maximum_fusion.t0), channel_id=1, source_target_pairs={{0,8},{1,3},{2,10},{3,5},{4,12},{5,7},{6,14},{7,1},{8,16},{9,11},{... | collective-permute-start | bytes 4915208 | tf_op jit(solution)/shard_map/ppermute | solution.py:35
  47.9 23.3 %collective-permute-start.11 = (bf16[800,256]{1,0:T(8,128)(2,1)}, bf16[800,256]{1,0:T(8,128)(2,1)}, u32[]{:S(2)}, u32[]{:S(2)}) collective-permute-start(bf16[800,256]{1,0:T(8,128)(2,1)} %get-tuple-element.46), channel_id=1, source_target_pairs={{0,2},{1,9},{2,4},{3,11},{4,6},{5,13},{6,0},{7,15},{8,10},{9,17},{... | collective-permute-start | bytes 1228808 | tf_op jit(solution)/shard_map/ppermute | solution.py:35
  53.4 17.8 %collective-permute-start.13 = (bf16[800,256]{1,0:T(8,128)(2,1)}, bf16[800,256]{1,0:T(8,128)(2,1)}, u32[]{:S(2)}, u32[]{:S(2)}) collective-permute-start(bf16[800,256]{1,0:T(8,128)(2,1)} %collective-permute-done.12), channel_id=1, source_target_pairs={{0,6},{1,25},{2,0},{3,27},{4,2},{5,29},{6,4},{7,31},{8,14},{9,1},{... | collective-permute-start | bytes 1228808 | tf_op jit(solution)/shard_map/ppermute | solution.py:35
  55.4 45.6 %collective-permute-start.5 = (bf16[4,800,256]{2,1,0:T(8,128)(2,1)S(1)}, bf16[4,800,256]{2,1,0:T(8,128)(2,1)}, u32[]{:S(2)}, u32[]{:S(2)}) collective-permute-start(bf16[4,800,256]{2,1,0:T(8,128)(2,1)S(1)} %pad_maximum_fusion.t0), channel_id=1, source_target_pairs={{0,24},{1,7},{2,26},{3,1},{4,28},{5,3},{6,30},{7,5},{8,0},{9,15},{... | collective-permute-start | bytes 4915208 | tf_op jit(solution)/shard_map/ppermute | solution.py:35
  70.9 30.1 %collective-permute-start.6 = (bf16[4,800,256]{2,1,0:T(8,128)(2,1)S(1)}, bf16[4,800,256]{2,1,0:T(8,128)(2,1)}, u32[]{:S(2)}, u32[]{:S(2)}) collective-permute-start(bf16[4,800,256]{2,1,0:T(8,128)(2,1)S(1)} %collective-permute-done.4.t1), channel_id=1, source_target_pairs={{0,8},{1,3},{2,10},{3,5},{4,12},{5,7},{6,14},{7,1},{8,16},{9,11},{... | collective-permute-start | bytes 4915208 | tf_op jit(solution)/shard_map/ppermute | solution.py:35
  73.8 14.9 %collective-permute-start.21 = (bf16[4,384,256]{2,1,0:T(8,128)(2,1)}, bf16[4,384,256]{2,1,0:T(8,128)(2,1)}, u32[]{:S(2)}, u32[]{:S(2)}) collective-permute-start(bf16[4,384,256]{2,1,0:T(8,128)(2,1)} %bitcast.17.t0), channel_id=1, source_target_pairs={{0,24},{1,7},{2,26},{3,1},{4,28},{5,3},{6,30},{7,5},{8,0},{9,15},{... | collective-permute-start | bytes 2359304 | tf_op jit(solution)/shard_map/ppermute | solution.py:35
  78.5 19.3 %collective-permute-start.15 = (bf16[4,416,256]{2,1,0:T(8,128)(2,1)}, bf16[4,416,256]{2,1,0:T(8,128)(2,1)}, u32[]{:S(2)}, u32[]{:S(2)}) collective-permute-start(bf16[4,416,256]{2,1,0:T(8,128)(2,1)} %bitcast.14.t0), channel_id=1, source_target_pairs={{0,24},{1,7},{2,26},{3,1},{4,28},{5,3},{6,30},{7,5},{8,0},{9,15},{... | collective-permute-start | bytes 2555912 | tf_op jit(solution)/shard_map/ppermute | solution.py:35
  88.6 41.0 %collective-permute-start.20 = (bf16[4,384,256]{2,1,0:T(8,128)(2,1)}, bf16[4,384,256]{2,1,0:T(8,128)(2,1)}, u32[]{:S(2)}, u32[]{:S(2)}) collective-permute-start(bf16[4,384,256]{2,1,0:T(8,128)(2,1)} %bitcast.17.t0), channel_id=1, source_target_pairs={{0,8},{1,3},{2,10},{3,5},{4,12},{5,7},{6,14},{7,1},{8,16},{9,11},{... | collective-permute-start | bytes 2359304 | tf_op jit(solution)/shard_map/ppermute | solution.py:35
  97.8 31.9 %collective-permute-start.22 = (bf16[4,384,256]{2,1,0:T(8,128)(2,1)}, bf16[4,384,256]{2,1,0:T(8,128)(2,1)}, u32[]{:S(2)}, u32[]{:S(2)}) collective-permute-start(bf16[4,384,256]{2,1,0:T(8,128)(2,1)} %collective-permute-done.21.t2), channel_id=1, source_target_pairs={{0,24},{1,7},{2,26},{3,1},{4,28},{5,3},{6,30},{7,5},{8,0},{9,15},{... | collective-permute-start | bytes 2359304 | tf_op jit(solution)/shard_map/ppermute | solution.py:35
  101.0 37.7 %collective-permute-start.14 = (bf16[4,416,256]{2,1,0:T(8,128)(2,1)}, bf16[4,416,256]{2,1,0:T(8,128)(2,1)}, u32[]{:S(2)}, u32[]{:S(2)}) collective-permute-start(bf16[4,416,256]{2,1,0:T(8,128)(2,1)} %bitcast.14.t0), channel_id=1, source_target_pairs={{0,8},{1,3},{2,10},{3,5},{4,12},{5,7},{6,14},{7,1},{8,16},{9,11},{... | collective-permute-start | bytes 2555912 | tf_op jit(solution)/shard_map/ppermute | solution.py:35
  101.1 39.6 %collective-permute-start.16 = (bf16[4,416,256]{2,1,0:T(8,128)(2,1)}, bf16[4,416,256]{2,1,0:T(8,128)(2,1)}, u32[]{:S(2)}, u32[]{:S(2)}) collective-permute-start(bf16[4,416,256]{2,1,0:T(8,128)(2,1)} %collective-permute-done.15.t2), channel_id=1, source_target_pairs={{0,24},{1,7},{2,26},{3,1},{4,28},{5,3},{6,30},{7,5},{8,0},{9,15},{... | collective-permute-start | bytes 2555912 | tf_op jit(solution)/shard_map/ppermute | solution.py:35
  125.8 24.4 %collective-permute-start.10 = (s16[2,200,512]{2,1,0:T(8,128)(2,1)S(1)}, s16[2,200,512]{2,1,0:T(8,128)(2,1)S(1)}, u32[]{:S(2)}, u32[]{:S(2)}) collective-permute-start(s16[2,200,512]{2,1,0:T(8,128)(2,1)S(1)} %get-tuple-element.26), channel_id=1, source_target_pairs={{0,96},{32,0},{64,32},{96,64},{1,97},{33,1},{65,33},{97,65},{2,98}... | collective-permute-start | bytes 1228808 | tf_op jit(solution)/shard_map/ppermute | solution.py:43
  129.6 24.1 %collective-permute-start.8 = (s16[2,200,512]{2,1,0:T(8,128)(2,1)}, s16[2,200,512]{2,1,0:T(8,128)(2,1)S(1)}, u32[]{:S(2)}, u32[]{:S(2)}) collective-permute-start(s16[2,200,512]{2,1,0:T(8,128)(2,1)} %get-tuple-element.24), channel_id=1, source_target_pairs={{0,32},{32,64},{64,96},{96,0},{1,33},{33,65},{65,97},{97,1},{2,34}... | collective-permute-start | bytes 1228808 | tf_op jit(solution)/shard_map/ppermute | solution.py:43
  129.6 24.1 %collective-permute-start.9 = (s16[2,200,512]{2,1,0:T(8,128)(2,1)S(1)}, s16[2,200,512]{2,1,0:T(8,128)(2,1)S(1)}, u32[]{:S(2)}, u32[]{:S(2)}) collective-permute-start(s16[2,200,512]{2,1,0:T(8,128)(2,1)S(1)} %get-tuple-element.25), channel_id=1, source_target_pairs={{0,64},{32,96},{64,0},{96,32},{1,65},{33,97},{65,1},{97,33},{2,66}... | collective-permute-start | bytes 1228808 | tf_op jit(solution)/shard_map/ppermute | solution.py:43
  138.7 17.1 %collective-permute-start.23 = (s16[2,96,512]{2,1,0:T(8,128)(2,1)S(1)}, s16[2,96,512]{2,1,0:T(8,128)(2,1)S(1)}, u32[]{:S(2)}, u32[]{:S(2)}) collective-permute-start(s16[2,96,512]{2,1,0:T(8,128)(2,1)S(1)} %get-tuple-element.34), channel_id=1, source_target_pairs={{0,32},{32,64},{64,96},{96,0},{1,33},{33,65},{65,97},{97,1},{2,34}... | collective-permute-start | bytes 589832 | tf_op jit(solution)/shard_map/ppermute | solution.py:43
  140.7 16.4 %collective-permute-start.24 = (s16[2,96,512]{2,1,0:T(8,128)(2,1)S(1)}, s16[2,96,512]{2,1,0:T(8,128)(2,1)S(1)}, u32[]{:S(2)}, u32[]{:S(2)}) collective-permute-start(s16[2,96,512]{2,1,0:T(8,128)(2,1)S(1)} %get-tuple-element.35), channel_id=1, source_target_pairs={{0,64},{32,96},{64,0},{96,32},{1,65},{33,97},{65,1},{97,33},{2,66}... | collective-permute-start | bytes 589832 | tf_op jit(solution)/shard_map/ppermute | solution.py:43
  150.2 10.9 %collective-permute-start.25 = (s16[2,96,512]{2,1,0:T(8,128)(2,1)S(1)}, s16[2,96,512]{2,1,0:T(8,128)(2,1)S(1)}, u32[]{:S(2)}, u32[]{:S(2)}) collective-permute-start(s16[2,96,512]{2,1,0:T(8,128)(2,1)S(1)} %get-tuple-element.36), channel_id=1, source_target_pairs={{0,96},{32,0},{64,32},{96,64},{1,97},{33,1},{65,33},{97,65},{2,98}... | collective-permute-start | bytes 589832 | tf_op jit(solution)/shard_map/ppermute | solution.py:43
  153.7 14.4 %collective-permute-start.17 = (s16[2,104,512]{2,1,0:T(8,128)(2,1)S(1)}, s16[2,104,512]{2,1,0:T(8,128)(2,1)S(1)}, u32[]{:S(2)}, u32[]{:S(2)}) collective-permute-start(s16[2,104,512]{2,1,0:T(8,128)(2,1)S(1)} %get-tuple-element.29), channel_id=1, source_target_pairs={{0,32},{32,64},{64,96},{96,0},{1,33},{33,65},{65,97},{97,1},{2,34}... | collective-permute-start | bytes 638984 | tf_op jit(solution)/shard_map/ppermute | solution.py:43
  153.8 14.4 %collective-permute-start.18 = (s16[2,104,512]{2,1,0:T(8,128)(2,1)S(1)}, s16[2,104,512]{2,1,0:T(8,128)(2,1)S(1)}, u32[]{:S(2)}, u32[]{:S(2)}) collective-permute-start(s16[2,104,512]{2,1,0:T(8,128)(2,1)S(1)} %get-tuple-element.30), channel_id=1, source_target_pairs={{0,64},{32,96},{64,0},{96,32},{1,65},{33,97},{65,1},{97,33},{2,66}... | collective-permute-start | bytes 638984 | tf_op jit(solution)/shard_map/ppermute | solution.py:43
  155.7 12.4 %collective-permute-start.19 = (s16[2,104,512]{2,1,0:T(8,128)(2,1)S(1)}, s16[2,104,512]{2,1,0:T(8,128)(2,1)S(1)}, u32[]{:S(2)}, u32[]{:S(2)}) collective-permute-start(s16[2,104,512]{2,1,0:T(8,128)(2,1)S(1)} %get-tuple-element.31), channel_id=1, source_target_pairs={{0,96},{32,0},{64,32},{96,64},{1,97},{33,1},{65,33},{97,65},{2,98}... | collective-permute-start | bytes 638984 | tf_op jit(solution)/shard_map/ppermute | solution.py:43
  157.1 12.6 %collective-permute-start.26 = (bf16[200,500]{1,0:T(8,128)(2,1)S(1)}, bf16[200,500]{1,0:T(8,128)(2,1)S(1)}, u32[]{:S(2)}, u32[]{:S(2)}) collective-permute-start(bf16[200,500]{1,0:T(8,128)(2,1)S(1)} %get-tuple-element.38), channel_id=1, source_target_pairs={{0,1},{1,0},{2,3},{3,2},{4,5},{5,4},{6,7},{7,6},{8,9},{9,8},{10,11... | collective-permute-start | bytes 600008 | tf_op jit(solution)/shard_map/ppermute | solution.py:39
  161.4 9.2 %collective-permute-start.28 = (bf16[96,500]{1,0:T(8,128)(2,1)S(1)}, bf16[96,500]{1,0:T(8,128)(2,1)S(1)}, u32[]{:S(2)}, u32[]{:S(2)}) collective-permute-start(bf16[96,500]{1,0:T(8,128)(2,1)S(1)} %get-tuple-element.40), channel_id=1, source_target_pairs={{0,1},{1,0},{2,3},{3,2},{4,5},{5,4},{6,7},{7,6},{8,9},{9,8},{10,11... | collective-permute-start | bytes 288008 | tf_op jit(solution)/shard_map/ppermute | solution.py:39
  (18 other events, 174.3 us)

commit v2 on v1

--- a/solution.py
+++ b/solution.py
@@ -11,11 +11,26 @@
 SHARD = 128
 COLS = 512
 OFFSETS = (0, -1, 1, 2)
-PARTS = (((0, 200),), ((0, 104), (104, 200)))
+CHUNKS = ((0, 0, 112), (1, 0, 112), (0, 112, 200), (1, 112, 200))
+TIES = {
+    "all1": ("own0",),
+    "all2": ("own1",),
+    "all3": ("own2",),
+    "code33": ("code11",),
+    "end0": ("own3",),
+    "end1": ("own3",),
+    "end2": ("own3",),
+    "far2": ("own0",),
+    "far3": ("code10", "own1"),
+    "minus2": ("minus0", "plus0"),
+    "minus3": ("minus1", "plus1"),
+    "plus2": ("minus0", "plus0"),
+    "plus3": ("minus1", "plus1"),
+}
 STEPS = 64.0
 LEAST = 2.0**-125
 TOP = 32766.0
-PARAMS = pltpu.CompilerParams(vmem_limit_bytes=24 * 1024 * 1024)
+PARAMS = pltpu.CompilerParams(vmem_limit_bytes=40 * 1024 * 1024)
 
 
 def ring_pairs(stage, hop):
@@ -43,6 +58,10 @@
     return lax.ppermute(value, "rep", [(i, (i + hop) % SIDE) for i in range(SIDE)])
 
 
+def after(value, *others):
+    return lax.optimization_barrier((value, *others))[0]
+
+
 def code_rows(acc, table, own, codes):
     _, _, rows, cols = acc.shape
     lane = lax.broadcasted_iota(jnp.int32, (rows, cols), 1)
@@ -61,27 +80,32 @@
 ):
     _, reps, rows, cols = acc.shape
     depth, width = w_own.shape[1:]
-    chips = t_buf.shape[0]
     block = table[16] * 2 + h
-    edges = [-(-chip_cols * SIDE * g // 16) * 16 for g in range(SIDE)] + [depth]
+    groups = [(0, 2), (2, 4), (4, 8), (8, 12), (12, 16)]
+    over = 2 * SHARD - chip_cols
+    edges = [0] + [-(-(chip_cols * low + over) // 16) * 16 for low, _ in groups[1:]] + [depth]
+    t_refs = (t0, t1, t2, t3)
     w_copies = []
-    for g in range(SIDE):
+    for g, (low, high) in enumerate(groups):
+        for chip in range(low, high):
+            place = table[21 + chip]
+            j, i = place // SIDE, place % SIDE
+            for arrival, t_ref in enumerate(t_refs):
+
+                @pl.when(j == arrival)
+                def _():
+                    pltpu.make_async_copy(t_ref.at[i], t_buf.at[chip], t_sem.at[chip]).start()
+
         span = pl.ds(edges[g], edges[g + 1] - edges[g])
         for side, w in enumerate((w_own, w_other)):
-            w_copies.append(pltpu.make_async_copy(w.at[block, span], w_buf.at[side, span], w_sem.at[g, side]))
-    for copy in w_copies[:2]:
-        copy.start()
-    for j, t_ref in enumerate((t0, t1, t2, t3)):
-        for i in range(SIDE):
-            chip = table[j * SIDE + i]
-            pltpu.make_async_copy(t_ref.at[i], t_buf.at[chip], t_sem.at[chip]).start()
-    for copy in w_copies[2:]:
-        copy.start()
+            copy = pltpu.make_async_copy(w.at[block, span], w_buf.at[side, span], w_sem.at[g, side])
+            copy.start()
+            w_copies.append(copy)
     tail = w_buf.shape[1] - depth
     for side in range(2):
         w_buf[side, depth:, :] = jnp.zeros((tail, width), w_buf.dtype)
-    for g in range(SIDE):
-        group = range(g * SIDE, (g + 1) * SIDE)
+    for g, (low, high) in enumerate(groups):
+        group = range(low, high)
         for copy in w_copies[2 * g : 2 * g + 2]:
             copy.wait()
         for chip in group:
@@ -118,7 +142,7 @@
                 pltpu.VMEM((2, depth + 16, width), jnp.bfloat16),
                 pltpu.VMEM((2, SIDE, rows, COLS), jnp.float32),
                 pltpu.SemaphoreType.DMA((chips,)),
-                pltpu.SemaphoreType.DMA((SIDE, 2)),
+                pltpu.SemaphoreType.DMA((5, 2)),
             ],
         ),
         out_shape=[jax.ShapeDtypeStruct(code_shape, jnp.float32)] + [jax.ShapeDtypeStruct(code_shape, jnp.int16)] * 3,
@@ -181,6 +205,17 @@
     return jnp.stack([energy_j, energy_b], axis=1)
 
 
+def place_of(core, y, x):
+    chip = jnp.arange(SIDE * SIDE, dtype=jnp.int32)
+    hop_y, hop_x = jnp.mod(chip // SIDE - y, SIDE), jnp.mod(chip % SIDE - x, SIDE)
+
+    def slot(hop):
+        return jnp.where(hop == 0, 0, jnp.where(hop == 1, 2, jnp.where(hop == 2, 3, 1)))
+
+    first, second = jnp.where(core == 0, hop_x, hop_y), jnp.where(core == 0, hop_y, hop_x)
+    return slot(second) * SIDE + slot(first)
+
+
 def shards(amplitudes, block_table, intermediate, slab_energy, slab_irrep, occ_energy, virt_energy):
     blocks, slab, virt, shard = amplitudes.shape
     width = intermediate.shape[2]
@@ -199,16 +234,15 @@
     kept = lax.dynamic_slice_in_dim(masked, core * mine, mine)
     given = lax.dynamic_slice_in_dim(masked, (1 - core) * mine, mine)
     got = swap_cores(given)
+    intermediate = after(intermediate, got)
     t = jnp.where(core == 0, jnp.concatenate([kept, got], axis=2), jnp.concatenate([got, kept], axis=2))
     t = jnp.pad(t, ((0, 0), (0, 0), (0, 2 * SHARD - 2 * shard)))
-    w_other = swap_cores(intermediate)
-
     near = (jnp.array(OFFSETS, jnp.int32)[None, :], jnp.array(OFFSETS, jnp.int32)[:, None])
     x_chip = jnp.where(core == 0, near[0], near[1])
     y_chip = jnp.where(core == 0, near[1], near[0])
     chips = jnp.mod(y + y_chip, SIDE) * SIDE + jnp.mod(x + x_chip, SIDE)
     table = jnp.concatenate(
-        [chips.reshape(-1), core[None], jnp.mod(rep + jnp.arange(SIDE, dtype=jnp.int32), SIDE)]
+        [chips.reshape(-1), core[None], jnp.mod(rep + jnp.arange(SIDE, dtype=jnp.int32), SIDE), place_of(core, y, x)]
     ).astype(jnp.int32)
 
     my_h = core * mine + jnp.arange(mine, dtype=jnp.int32)
@@ -217,23 +251,55 @@
         [col_energies(my_h, c, width, occ_energy, virt_energy) for c in (con, jnp.bitwise_xor(con, 1))], axis=1
     )
 
-    kept, got = [], []
-    for h in range(mine):
-        before, after = ring(t[h], 0, 1), ring(t[h], 0, -1)
-        hop = 1 if h == 0 else -1
-        far = ring(before if h == 0 else after, 0, hop)
-        row = jnp.stack([t[h], before, after, far]).reshape(SIDE, SIDE, per_rep, 2 * SHARD)
-        for first, last in PARTS[h]:
-            here = row[:, :, first:last].reshape(SIDE, -1, 2 * SHARD)
-            row_before, row_after = ring(here, 1, 1), ring(here, 1, -1)
-            row_far = ring(row_before if h == 0 else row_after, 1, hop)
-            t_parts = (here, row_before, row_after, row_far)
-            own, *codes = multiply(table, h, 2 * shard, t_parts, intermediate, w_other)
-            codes = [to_replica(code, hops + 1) for hops, code in enumerate(codes)]
-            out_own, out_other = finish(own, codes, rows_e[h, first:last], cols_e[h], width)
-            kept.append(out_own)
-            got.append(swap_cores(out_other))
-
+    table = after(table, rows_e, cols_e)
+    known = {}
+
+    def tied(name, value):
+        return after(value, *[node(other) for other in TIES[name]]) if name in TIES else value
+
+    def node(name):
+        if name not in known:
+            known[name] = build(name)
+        return known[name]
+
+    def build(name):
+        kind, k = name[:-1], int(name[-1])
+        if kind == "w":
+            return swap_cores(tied(name, intermediate))
+        if kind == "t":
+            return t[k]
+        if kind == "both":
+            return ring(tied(name, t), 0, 1 if k == 0 else -1)
+        if kind == "side":
+            return ring(tied(name, node(f"both{k}")[k]), 0, 1 if k == 0 else -1)
+        if kind == "row":
+            row = jnp.stack([t[k], node("both0")[k], node("both1")[k], node(f"side{k}")])
+            return row.reshape(SIDE, SIDE, per_rep, 2 * SHARD)
+        h, first, last = CHUNKS[k]
+        if kind == "here":
+            return node(f"row{h}")[:, :, first:last].reshape(SIDE, -1, 2 * SHARD)
+        if kind == "plus":
+            return ring(tied(name, node(f"here{k}")), 1, 1)
+        if kind == "minus":
+            return ring(tied(name, node(f"here{k}")), 1, -1)
+        if kind == "far":
+            return ring(tied(name, node(f"plus{k}" if h == 0 else f"minus{k}")), 1, 1 if h == 0 else -1)
+        if kind == "all":
+            parts = [node(f"{part}{k}") for part in ("here", "plus", "minus", "far")]
+            return multiply(tied(name, table), h, 2 * shard, parts, intermediate, node("w0"))
+        if kind == "own":
+            return node(f"all{k}")[0]
+        if kind[:-1] == "code":
+            hop = int(kind[-1])
+            return to_replica(tied(name, node(f"all{k}")[hop]), hop)
+        codes = [node(f"code{hop}{k}") for hop in (1, 2, 3)]
+        return finish(tied(name, node(f"own{k}")), codes, rows_e[h, first:last], cols_e[h], width)
+
+    done = {}
+    for k, (h, first, last) in enumerate(CHUNKS):
+        out_own, out_other = node(f"end{k}")
+        done[h, first] = out_own, swap_cores(out_other)
+    kept, got = [done[key][0] for key in sorted(done)], [done[key][1] for key in sorted(done)]
     kept, got = jnp.concatenate(kept), jnp.concatenate(got)
     out = jnp.where(core == 0, jnp.concatenate([kept, got]), jnp.concatenate([got, kept]))
     return out.reshape(blocks, slab // SIDE, virt, width)

time: 173 us -> 140 us (0.81)
  waiting for transfers between devices: 75.6 us -> 41.5 us
  starting transfers between devices: 42.5 us -> 48.1 us
  local copies, waits for them, and re-layouts: 14.7 us -> 11.2 us
    ppermute x5 -> x6, waiting for transfers between devices: 23 us -> 3.56 us  [swap_cores(): lax.ppermute(value, 'con', [(i, i ^ 1) for i in range(2 * SIDE * SIDE)])]
    ppermute x15 -> x16, waiting for transfers between devices: 48.9 us -> 32.2 us  [ring(): return lax.ppermute(value, 'con', ring_pairs(stage, hop))]
    unnamed x33 -> x64, local copies, waits for them, and re-layouts: 8.66 us -> 4.25 us
    ppermute x15 -> x16, starting transfers between devices: 18.2 us -> 21.6 us  [ring(): return lax.ppermute(value, 'con', ring_pairs(stage, hop))]
    ppermute x9 -> x12, waiting for transfers between devices: 3.7 us -> 5.75 us  [to_replica(): lax.ppermute(value, 'rep', [(i, (i + hop) % SIDE) for i in range(SIDE)])]
    ppermute x9 -> x12, starting transfers between devices: 13.9 us -> 15.7 us  [to_replica(): lax.ppermute(value, 'rep', [(i, (i + hop) % SIDE) for i in range(SIDE)])]
    slice x2 -> x5, local copies, waits for them, and re-layouts: 1.97 us -> 3.71 us  [the longest x1 1.96 us: build(): node('both0')[k]]
    pallas_call x3 -> x4, Pallas kernels: 29.4 us -> 30 us  [multiply(): pl.pallas_call(functools.partial(product_kernel, h, chip_cols), grid_spec...]
  transfers between devices with their start and end apart: 29 -> 34, of which waited for: 11 -> 9; matrix products, arithmetic and copies ran while one was open for 8% -> 7% of each run, Pallas kernels for 18% -> 22%
where the time goes in v2:
time: 140 us
  starting transfers between devices  48.1 us (34%)
  waiting for transfers between devices  41.5 us (30%)
  Pallas kernels  31.2 us (22%)
  local copies, waits for them, and re-layouts  11.2 us (8%)
  other arithmetic  7.32 us (5%)
    ppermute x16, waiting for transfers between devices, ring(): return lax.ppermute(value, 'con', ring_pairs(stage, hop))  32.2 us
    pallas_call x4, Pallas kernels, multiply(): pl.pallas_call(functools.partial(product_kernel, h, chip_cols), grid_spec...  30 us
    ppermute x16, starting transfers between devices, ring(): return lax.ppermute(value, 'con', ring_pairs(stage, hop))  21.6 us
    ppermute x12, starting transfers between devices, to_replica(): lax.ppermute(value, 'rep', [(i, (i + hop) % SIDE) for i in range(SIDE)])  15.7 us
    ppermute x6, starting transfers between devices, swap_cores(): lax.ppermute(value, 'con', [(i, i ^ 1) for i in range(2 * SIDE * SIDE)])  10.8 us
    ppermute x12, waiting for transfers between devices, to_replica(): lax.ppermute(value, 'rep', [(i, (i + hop) % SIDE) for i in range(SIDE)])  5.75 us
    unnamed x64, local copies, waits for them, and re-layouts  4.25 us
    ppermute x6, waiting for transfers between devices, swap_cores(): lax.ppermute(value, 'con', [(i, i ^ 1) for i in range(2 * SIDE * SIDE)])  3.56 us
  transfers between devices with their start and end apart: 34, of which 9 were waited for; matrix products, arithmetic and copies ran while one was open for 7% of the time, Pallas kernels for 22%

profile of v2, /device:TPU:1, one launch (start us, length us, event | category | flops | bytes accessed | tf_op | source)
XLA Modules:
  0.0 140.1 jit_solution(4805660335171860187)
XLA Ops:
  10.1 9.7 %collective-permute-done.1 = bf16[2,800,256]{2,1,0:T(8,128)(2,1)} collective-permute-done((bf16[2,800,256]{2,1,0:T(8,128)(2,1)S(1)}, bf16[2,800,256]{2,1,0:T(8,128)(2,1)}, u32[]{:S(2)}, u32[]{:S(2)}) %collective-permute-start.1) | collective-permute-done | bytes 819232 | tf_op jit(solution)/shard_map/ppermute | solution.py:50
  19.8 2.0 %fusion.38 = (bf16[1,800,256]{2,1,0:T(8,128)(2,1)S(1)}, bf16[800,256]{1,0:T(8,128)(2,1)}, bf16[1,800,256]{2,1,0:T(8,128)(2,1)S(1)}) fusion(bf16[2,800,256]{2,1,0:T(8,128)(2,1)} %collective-permute-done.1), kind=kLoop, calls=%fused_computation.144 | loop fusion | bytes 2048000 | tf_op jit(solution)/shard_map/slice | solution.py:276
  23.7 2.7 %collective-permute-start.8 = (bf16[800,256]{1,0:T(8,128)(2,1)S(1)}, bf16[800,256]{1,0:T(8,128)(2,1)S(1)}, u32[]{:S(2)}, u32[]{:S(2)}) collective-permute-start(bf16[800,256]{1,0:T(8,128)(2,1)S(1)} %get-tuple-element.89), channel_id=1, source_target_pairs={{0,6},{1,25},{2,0},{3,27},{4,2},{5,29},{6,4},{7,31},{8,14},{9,1},{... | collective-permute-start | bytes 1228808 | tf_op jit(solution)/shard_map/ppermute | solution.py:50
  26.4 3.8 %collective-permute-done.3 = bf16[800,256]{1,0:T(8,128)(2,1)S(1)} collective-permute-done((bf16[800,256]{1,0:T(8,128)(2,1)}, bf16[800,256]{1,0:T(8,128)(2,1)S(1)}, u32[]{:S(2)}, u32[]{:S(2)}) %collective-permute-start.3) | collective-permute-done | bytes 409632 | tf_op jit(solution)/shard_map/ppermute | solution.py:50
  33.0 2.1 %collective-permute-start.10 = (bf16[4,448,256]{2,1,0:T(8,128)(2,1)S(1)}, bf16[4,448,256]{2,1,0:T(8,128)(2,1)}, u32[]{:S(2)}, u32[]{:S(2)}) collective-permute-start(bf16[4,448,256]{2,1,0:T(8,128)(2,1)S(1)} %bitcast.36), channel_id=1, source_target_pairs={{0,24},{1,7},{2,26},{3,1},{4,28},{5,3},{6,30},{7,5},{8,0},{9,15},{... | collective-permute-start | bytes 2752520 | tf_op jit(solution)/shard_map/ppermute | solution.py:50
  36.8 8.4 %collective-permute-done.4.t1 = bf16[4,448,256]{2,1,0:T(8,128)(2,1)} collective-permute-done((bf16[4,448,256]{2,1,0:T(8,128)(2,1)S(1)}, bf16[4,448,256]{2,1,0:T(8,128)(2,1)}, u32[]{:S(2)}, u32[]{:S(2)}) %collective-permute-start.4) | collective-permute-done | bytes 917536 | tf_op jit(solution)/shard_map/ppermute | solution.py:50
  46.1 2.9 %collective-permute-start.11 = (bf16[4,448,256]{2,1,0:T(8,128)(2,1)}, bf16[4,448,256]{2,1,0:T(8,128)(2,1)S(1)}, u32[]{:S(2)}, u32[]{:S(2)}) collective-permute-start(bf16[4,448,256]{2,1,0:T(8,128)(2,1)} %collective-permute-done.10.t2), channel_id=1, source_target_pairs={{0,24},{1,7},{2,26},{3,1},{4,28},{5,3},{6,30},{7,5},{8,0},{9,15},{... | collective-permute-start | bytes 2752520 | tf_op jit(solution)/shard_map/ppermute | solution.py:50
  50.1 5.5 %collective-permute-done.5.t2 = bf16[4,448,256]{2,1,0:T(8,128)(2,1)} collective-permute-done((bf16[4,448,256]{2,1,0:T(8,128)(2,1)S(1)}, bf16[4,448,256]{2,1,0:T(8,128)(2,1)}, u32[]{:S(2)}, u32[]{:S(2)}) %collective-permute-start.5) | collective-permute-done | bytes 917536 | tf_op jit(solution)/shard_map/ppermute | solution.py:50
  58.0 2.1 %collective-permute-start.16 = (bf16[4,352,256]{2,1,0:T(8,128)(2,1)S(1)}, bf16[4,352,256]{2,1,0:T(8,128)(2,1)}, u32[]{:S(2)}, u32[]{:S(2)}) collective-permute-start(bf16[4,352,256]{2,1,0:T(8,128)(2,1)S(1)} %bitcast.39), channel_id=1, source_target_pairs={{0,24},{1,7},{2,26},{3,1},{4,28},{5,3},{6,30},{7,5},{8,0},{9,15},{... | collective-permute-start | bytes 2162696 | tf_op jit(solution)/shard_map/ppermute | solution.py:50
  60.2 4.7 %collective-permute-done.6.t3 = bf16[4,448,256]{2,1,0:T(8,128)(2,1)} collective-permute-done((bf16[4,448,256]{2,1,0:T(8,128)(2,1)}, bf16[4,448,256]{2,1,0:T(8,128)(2,1)}, u32[]{:S(2)}, u32[]{:S(2)}) %collective-permute-start.6) | collective-permute-done | bytes 917536 | tf_op jit(solution)/shard_map/ppermute | solution.py:50
  64.9 2.7 %collective-permute-start.13 = (bf16[4,352,256]{2,1,0:T(8,128)(2,1)S(1)}, bf16[4,352,256]{2,1,0:T(8,128)(2,1)}, u32[]{:S(2)}, u32[]{:S(2)}) collective-permute-start(bf16[4,352,256]{2,1,0:T(8,128)(2,1)S(1)} %bitcast.43), channel_id=1, source_target_pairs={{0,24},{1,7},{2,26},{3,1},{4,28},{5,3},{6,30},{7,5},{8,0},{9,15},{... | collective-permute-start | bytes 2162696 | tf_op jit(solution)/shard_map/ppermute | solution.py:50
  67.6 7.6 %shard_map.91 = (f32[2,112,512]{2,1,0:T(8,128)S(1)}, s16[2,112,512]{2,1,0:T(8,128)(2,1)S(1)}, s16[2,112,512]{2,1,0:T(8,128)(2,1)S(1)}, s16[2,112,512]{2,1,0:T(8,128)(2,1)S(1)}) custom-call(s32[37]{0:T(128)S(1)} %pad_add_fusion.table, bf16[4,448,256]{2,1,0:T(8,128)(2,1)S(1)} %bitcast.35, bf16[4,448,256]{2,1,0:T(8,128)(2,1)} %collective-permute-done.4.t1, ...), custom_call_target="tpu_custom_call" | custom-call | flops 3584000000 | bytes 24000000 | tf_op jit(solution)/shard_map/pallas_call | solution.py:133
  76.9 8.6 %shard_map.92 = (f32[2,112,512]{2,1,0:T(8,128)S(1)}, s16[2,112,512]{2,1,0:T(8,128)(2,1)S(1)}, s16[2,112,512]{2,1,0:T(8,128)(2,1)S(1)}, s16[2,112,512]{2,1,0:T(8,128)(2,1)S(1)}) custom-call(s32[37]{0:T(128)S(1)} %pad_add_fusion.table, bf16[4,448,256]{2,1,0:T(8,128)(2,1)S(1)} %bitcast.38, bf16[4,448,256]{2,1,0:T(8,128)(2,1)} %collective-permute-done.9.t1, ...), custom_call_target="tpu_custom_call" | custom-call | flops 3584000000 | bytes 24000000 | tf_op jit(solution)/shard_map/pallas_call | solution.py:133
  88.4 2.7 %collective-permute-start.18 = (bf16[4,352,256]{2,1,0:T(8,128)(2,1)}, bf16[4,352,256]{2,1,0:T(8,128)(2,1)S(1)}, u32[]{:S(2)}, u32[]{:S(2)}) collective-permute-start(bf16[4,352,256]{2,1,0:T(8,128)(2,1)} %collective-permute-done.16.t2), channel_id=1, source_target_pairs={{0,24},{1,7},{2,26},{3,1},{4,28},{5,3},{6,30},{7,5},{8,0},{9,15},{... | collective-permute-start | bytes 2162696 | tf_op jit(solution)/shard_map/ppermute | solution.py:50
  91.9 1.7 %collective-permute-start.24 = (s16[2,112,512]{2,1,0:T(8,128)(2,1)}, s16[2,112,512]{2,1,0:T(8,128)(2,1)S(1)}, u32[]{:S(2)}, u32[]{:S(2)}) collective-permute-start(s16[2,112,512]{2,1,0:T(8,128)(2,1)} %copy-done.10), channel_id=1, source_target_pairs={{0,32},{32,64},{64,96},{96,0},{1,33},{33,65},{65,97},{97,1},{2,34}... | collective-permute-start | bytes 688136 | tf_op jit(solution)/shard_map/ppermute | solution.py:58
  93.6 1.8 %collective-permute-start.19 = (s16[2,112,512]{2,1,0:T(8,128)(2,1)}, s16[2,112,512]{2,1,0:T(8,128)(2,1)S(1)}, u32[]{:S(2)}, u32[]{:S(2)}) collective-permute-start(s16[2,112,512]{2,1,0:T(8,128)(2,1)} %copy-done.9), channel_id=1, source_target_pairs={{0,64},{32,96},{64,0},{96,32},{1,65},{33,97},{65,1},{97,33},{2,66}... | collective-permute-start | bytes 688136 | tf_op jit(solution)/shard_map/ppermute | solution.py:58
  95.3 2.0 %collective-permute-start.20 = (s16[2,112,512]{2,1,0:T(8,128)(2,1)}, s16[2,112,512]{2,1,0:T(8,128)(2,1)S(1)}, u32[]{:S(2)}, u32[]{:S(2)}) collective-permute-start(s16[2,112,512]{2,1,0:T(8,128)(2,1)} %copy-done.8), channel_id=1, source_target_pairs={{0,96},{32,0},{64,32},{96,64},{1,97},{33,1},{65,33},{97,65},{2,98}... | collective-permute-start | bytes 688136 | tf_op jit(solution)/shard_map/ppermute | solution.py:58
  97.3 6.7 %shard_map.93 = (f32[2,88,512]{2,1,0:T(8,128)S(1)}, s16[2,88,512]{2,1,0:T(8,128)(2,1)S(1)}, s16[2,88,512]{2,1,0:T(8,128)(2,1)S(1)}, s16[2,88,512]{2,1,0:T(8,128)(2,1)S(1)}) custom-call(s32[37]{0:T(128)S(1)} %pad_add_fusion.table, bf16[4,352,256]{2,1,0:T(8,128)(2,1)S(1)} %bitcast.44, bf16[4,352,256]{2,1,0:T(8,128)(2,1)} %collective-permute-done.12.t1, ...), custom_call_target="tpu_custom_call" | custom-call | flops 2816000000 | bytes 24000000 | tf_op jit(solution)/shard_map/pallas_call | solution.py:133
  104.2 1.9 %collective-permute-start.26 = (s16[2,112,512]{2,1,0:T(8,128)(2,1)S(1)}, s16[2,112,512]{2,1,0:T(8,128)(2,1)S(1)}, u32[]{:S(2)}, u32[]{:S(2)}) collective-permute-start(s16[2,112,512]{2,1,0:T(8,128)(2,1)S(1)} %copy-done.5), channel_id=1, source_target_pairs={{0,96},{32,0},{64,32},{96,64},{1,97},{33,1},{65,33},{97,65},{2,98}... | collective-permute-start | bytes 688136 | tf_op jit(solution)/shard_map/ppermute | solution.py:58
  106.0 2.5 %collective-permute-start.22 = (s16[2,88,512]{2,1,0:T(8,128)(2,1)S(1)}, s16[2,88,512]{2,1,0:T(8,128)(2,1)S(1)}, u32[]{:S(2)}, u32[]{:S(2)}) collective-permute-start(s16[2,88,512]{2,1,0:T(8,128)(2,1)S(1)} %get-tuple-element.62), channel_id=1, source_target_pairs={{0,64},{32,96},{64,0},{96,32},{1,65},{33,97},{65,1},{97,33},{2,66}... | collective-permute-start | bytes 540680 | tf_op jit(solution)/shard_map/ppermute | solution.py:58
  109.3 7.2 %shard_map.94 = (f32[2,88,512]{2,1,0:T(8,128)S(1)}, s16[2,88,512]{2,1,0:T(8,128)(2,1)S(1)}, s16[2,88,512]{2,1,0:T(8,128)(2,1)S(1)}, s16[2,88,512]{2,1,0:T(8,128)(2,1)S(1)}) custom-call(s32[37]{0:T(128)S(1)} %pad_add_fusion.table, bf16[4,352,256]{2,1,0:T(8,128)(2,1)S(1)} %bitcast.41, bf16[4,352,256]{2,1,0:T(8,128)(2,1)} %collective-permute-done.15.t1, ...), custom_call_target="tpu_custom_call" | custom-call | flops 2816000000 | bytes 24000000 | tf_op jit(solution)/shard_map/pallas_call | solution.py:133
  116.8 6.7 %collective-permute-start.30 = (bf16[112,500]{1,0:T(8,128)(2,1)S(1)}, bf16[112,500]{1,0:T(8,128)(2,1)S(1)}, u32[]{:S(2)}, u32[]{:S(2)}) collective-permute-start(bf16[112,500]{1,0:T(8,128)(2,1)S(1)} %get-tuple-element.75), channel_id=1, source_target_pairs={{0,1},{1,0},{2,3},{3,2},{4,5},{5,4},{6,7},{7,6},{8,9},{9,8},{10,11... | collective-permute-start | bytes 336008 | tf_op jit(solution)/shard_map/ppermute | solution.py:54
  125.6 1.8 %collective-permute-start.28 = (s16[2,88,512]{2,1,0:T(8,128)(2,1)S(1)}, s16[2,88,512]{2,1,0:T(8,128)(2,1)S(1)}, u32[]{:S(2)}, u32[]{:S(2)}) collective-permute-start(s16[2,88,512]{2,1,0:T(8,128)(2,1)S(1)} %get-tuple-element.71), channel_id=1, source_target_pairs={{0,64},{32,96},{64,0},{96,32},{1,65},{33,97},{65,1},{97,33},{2,66}... | collective-permute-start | bytes 540680 | tf_op jit(solution)/shard_map/ppermute | solution.py:58
  130.0 5.7 %collective-permute-done.28.code2 = s16[2,88,512]{2,1,0:T(8,128)(2,1)S(1)} collective-permute-done((s16[2,88,512]{2,1,0:T(8,128)(2,1)S(1)}, s16[2,88,512]{2,1,0:T(8,128)(2,1)S(1)}, u32[]{:S(2)}, u32[]{:S(2)}) %collective-permute-start.28) | collective-permute-done | bytes 180256 | tf_op jit(solution)/shard_map/ppermute | solution.py:58
  (173 shorter events, 36.0 us)
Async XLA Ops:
  5.5 59.4 %collective-permute-start.7 = (bf16[4,4000,500]{2,1,0:T(8,128)(2,1)}, bf16[4,4000,500]{2,1,0:T(8,128)(2,1)}, u32[]{:S(2)}, u32[]{:S(2)}) collective-permute-start(bf16[4,4000,500]{2,1,0:T(8,128)(2,1)} %w_own.3), channel_id=1, source_target_pairs={{0,1},{1,0},{2,3},{3,2},{4,5},{5,4},{6,7},{7,6},{8,9},{9,8},{10,11... | collective-permute-start | bytes 48000008 | tf_op jit(solution)/shard_map/ppermute | solution.py:54
  6.8 13.0 %collective-permute-start.1 = (bf16[2,800,256]{2,1,0:T(8,128)(2,1)S(1)}, bf16[2,800,256]{2,1,0:T(8,128)(2,1)}, u32[]{:S(2)}, u32[]{:S(2)}) collective-permute-start(bf16[2,800,256]{2,1,0:T(8,128)(2,1)S(1)} %pad.4), channel_id=1, source_target_pairs={{0,2},{1,9},{2,4},{3,11},{4,6},{5,13},{6,0},{7,15},{8,10},{9,17},{... | collective-permute-start | bytes 2457608 | tf_op jit(solution)/shard_map/ppermute | solution.py:50
  8.4 13.8 %collective-permute-start.2 = (bf16[2,800,256]{2,1,0:T(8,128)(2,1)S(1)}, bf16[2,800,256]{2,1,0:T(8,128)(2,1)}, u32[]{:S(2)}, u32[]{:S(2)}) collective-permute-start(bf16[2,800,256]{2,1,0:T(8,128)(2,1)S(1)} %pad.4), channel_id=1, source_target_pairs={{0,6},{1,25},{2,0},{3,27},{4,2},{5,29},{6,4},{7,31},{8,14},{9,1},{... | collective-permute-start | bytes 2457608 | tf_op jit(solution)/shard_map/ppermute | solution.py:50
  31.3 13.9 %collective-permute-start.4 = (bf16[4,448,256]{2,1,0:T(8,128)(2,1)S(1)}, bf16[4,448,256]{2,1,0:T(8,128)(2,1)}, u32[]{:S(2)}, u32[]{:S(2)}) collective-permute-start(bf16[4,448,256]{2,1,0:T(8,128)(2,1)S(1)} %bitcast.33), channel_id=1, source_target_pairs={{0,8},{1,3},{2,10},{3,5},{4,12},{5,7},{6,14},{7,1},{8,16},{9,11},{... | collective-permute-start | bytes 2752520 | tf_op jit(solution)/shard_map/ppermute | solution.py:50
  33.0 13.1 %collective-permute-start.10 = (bf16[4,448,256]{2,1,0:T(8,128)(2,1)S(1)}, bf16[4,448,256]{2,1,0:T(8,128)(2,1)}, u32[]{:S(2)}, u32[]{:S(2)}) collective-permute-start(bf16[4,448,256]{2,1,0:T(8,128)(2,1)S(1)} %bitcast.36), channel_id=1, source_target_pairs={{0,24},{1,7},{2,26},{3,1},{4,28},{5,3},{6,30},{7,5},{8,0},{9,15},{... | collective-permute-start | bytes 2752520 | tf_op jit(solution)/shard_map/ppermute | solution.py:50
  35.2 20.4 %collective-permute-start.5 = (bf16[4,448,256]{2,1,0:T(8,128)(2,1)S(1)}, bf16[4,448,256]{2,1,0:T(8,128)(2,1)}, u32[]{:S(2)}, u32[]{:S(2)}) collective-permute-start(bf16[4,448,256]{2,1,0:T(8,128)(2,1)S(1)} %bitcast.34), channel_id=1, source_target_pairs={{0,24},{1,7},{2,26},{3,1},{4,28},{5,3},{6,30},{7,5},{8,0},{9,15},{... | collective-permute-start | bytes 2752520 | tf_op jit(solution)/shard_map/ppermute | solution.py:50
  36.6 21.4 %collective-permute-start.9 = (bf16[4,448,256]{2,1,0:T(8,128)(2,1)S(1)}, bf16[4,448,256]{2,1,0:T(8,128)(2,1)}, u32[]{:S(2)}, u32[]{:S(2)}) collective-permute-start(bf16[4,448,256]{2,1,0:T(8,128)(2,1)S(1)} %bitcast.37), channel_id=1, source_target_pairs={{0,8},{1,3},{2,10},{3,5},{4,12},{5,7},{6,14},{7,1},{8,16},{9,11},{... | collective-permute-start | bytes 2752520 | tf_op jit(solution)/shard_map/ppermute | solution.py:50
  45.2 19.7 %collective-permute-start.6 = (bf16[4,448,256]{2,1,0:T(8,128)(2,1)}, bf16[4,448,256]{2,1,0:T(8,128)(2,1)}, u32[]{:S(2)}, u32[]{:S(2)}) collective-permute-start(bf16[4,448,256]{2,1,0:T(8,128)(2,1)} %collective-permute-done.4.t1), channel_id=1, source_target_pairs={{0,8},{1,3},{2,10},{3,5},{4,12},{5,7},{6,14},{7,1},{8,16},{9,11},{... | collective-permute-start | bytes 2752520 | tf_op jit(solution)/shard_map/ppermute | solution.py:50
  46.1 30.8 %collective-permute-start.11 = (bf16[4,448,256]{2,1,0:T(8,128)(2,1)}, bf16[4,448,256]{2,1,0:T(8,128)(2,1)S(1)}, u32[]{:S(2)}, u32[]{:S(2)}) collective-permute-start(bf16[4,448,256]{2,1,0:T(8,128)(2,1)} %collective-permute-done.10.t2), channel_id=1, source_target_pairs={{0,24},{1,7},{2,26},{3,1},{4,28},{5,3},{6,30},{7,5},{8,0},{9,15},{... | collective-permute-start | bytes 2752520 | tf_op jit(solution)/shard_map/ppermute | solution.py:50
  55.6 19.6 %collective-permute-start.12 = (bf16[4,352,256]{2,1,0:T(8,128)(2,1)S(1)}, bf16[4,352,256]{2,1,0:T(8,128)(2,1)}, u32[]{:S(2)}, u32[]{:S(2)}) collective-permute-start(bf16[4,352,256]{2,1,0:T(8,128)(2,1)S(1)} %bitcast.42), channel_id=1, source_target_pairs={{0,8},{1,3},{2,10},{3,5},{4,12},{5,7},{6,14},{7,1},{8,16},{9,11},{... | collective-permute-start | bytes 2162696 | tf_op jit(solution)/shard_map/ppermute | solution.py:50
  58.0 30.3 %collective-permute-start.16 = (bf16[4,352,256]{2,1,0:T(8,128)(2,1)S(1)}, bf16[4,352,256]{2,1,0:T(8,128)(2,1)}, u32[]{:S(2)}, u32[]{:S(2)}) collective-permute-start(bf16[4,352,256]{2,1,0:T(8,128)(2,1)S(1)} %bitcast.39), channel_id=1, source_target_pairs={{0,24},{1,7},{2,26},{3,1},{4,28},{5,3},{6,30},{7,5},{8,0},{9,15},{... | collective-permute-start | bytes 2162696 | tf_op jit(solution)/shard_map/ppermute | solution.py:50
  64.9 39.1 %collective-permute-start.15 = (bf16[4,352,256]{2,1,0:T(8,128)(2,1)S(1)}, bf16[4,352,256]{2,1,0:T(8,128)(2,1)}, u32[]{:S(2)}, u32[]{:S(2)}) collective-permute-start(bf16[4,352,256]{2,1,0:T(8,128)(2,1)S(1)} %bitcast.40), channel_id=1, source_target_pairs={{0,8},{1,3},{2,10},{3,5},{4,12},{5,7},{6,14},{7,1},{8,16},{9,11},{... | collective-permute-start | bytes 2162696 | tf_op jit(solution)/shard_map/ppermute | solution.py:50
  64.9 28.7 %collective-permute-start.13 = (bf16[4,352,256]{2,1,0:T(8,128)(2,1)S(1)}, bf16[4,352,256]{2,1,0:T(8,128)(2,1)}, u32[]{:S(2)}, u32[]{:S(2)}) collective-permute-start(bf16[4,352,256]{2,1,0:T(8,128)(2,1)S(1)} %bitcast.43), channel_id=1, source_target_pairs={{0,24},{1,7},{2,26},{3,1},{4,28},{5,3},{6,30},{7,5},{8,0},{9,15},{... | collective-permute-start | bytes 2162696 | tf_op jit(solution)/shard_map/ppermute | solution.py:50
  75.2 13.2 %collective-permute-start.17 = (s16[2,112,512]{2,1,0:T(8,128)(2,1)S(1)}, s16[2,112,512]{2,1,0:T(8,128)(2,1)S(1)}, u32[]{:S(2)}, u32[]{:S(2)}) collective-permute-start(s16[2,112,512]{2,1,0:T(8,128)(2,1)S(1)} %get-tuple-element.53), channel_id=1, source_target_pairs={{0,32},{32,64},{64,96},{96,0},{1,33},{33,65},{65,97},{97,1},{2,34}... | collective-permute-start | bytes 688136 | tf_op jit(solution)/shard_map/ppermute | solution.py:58
  76.9 18.4 %collective-permute-start.14 = (bf16[4,352,256]{2,1,0:T(8,128)(2,1)}, bf16[4,352,256]{2,1,0:T(8,128)(2,1)}, u32[]{:S(2)}, u32[]{:S(2)}) collective-permute-start(bf16[4,352,256]{2,1,0:T(8,128)(2,1)} %collective-permute-done.12.t1), channel_id=1, source_target_pairs={{0,8},{1,3},{2,10},{3,5},{4,12},{5,7},{6,14},{7,1},{8,16},{9,11},{... | collective-permute-start | bytes 2162696 | tf_op jit(solution)/shard_map/ppermute | solution.py:50
  88.4 20.2 %collective-permute-start.18 = (bf16[4,352,256]{2,1,0:T(8,128)(2,1)}, bf16[4,352,256]{2,1,0:T(8,128)(2,1)S(1)}, u32[]{:S(2)}, u32[]{:S(2)}) collective-permute-start(bf16[4,352,256]{2,1,0:T(8,128)(2,1)} %collective-permute-done.16.t2), channel_id=1, source_target_pairs={{0,24},{1,7},{2,26},{3,1},{4,28},{5,3},{6,30},{7,5},{8,0},{9,15},{... | collective-permute-start | bytes 2162696 | tf_op jit(solution)/shard_map/ppermute | solution.py:50
  91.9 12.3 %collective-permute-start.24 = (s16[2,112,512]{2,1,0:T(8,128)(2,1)}, s16[2,112,512]{2,1,0:T(8,128)(2,1)S(1)}, u32[]{:S(2)}, u32[]{:S(2)}) collective-permute-start(s16[2,112,512]{2,1,0:T(8,128)(2,1)} %copy-done.10), channel_id=1, source_target_pairs={{0,32},{32,64},{64,96},{96,0},{1,33},{33,65},{65,97},{97,1},{2,34}... | collective-permute-start | bytes 688136 | tf_op jit(solution)/shard_map/ppermute | solution.py:58
  93.6 12.5 %collective-permute-start.19 = (s16[2,112,512]{2,1,0:T(8,128)(2,1)}, s16[2,112,512]{2,1,0:T(8,128)(2,1)S(1)}, u32[]{:S(2)}, u32[]{:S(2)}) collective-permute-start(s16[2,112,512]{2,1,0:T(8,128)(2,1)} %copy-done.9), channel_id=1, source_target_pairs={{0,64},{32,96},{64,0},{96,32},{1,65},{33,97},{65,1},{97,33},{2,66}... | collective-permute-start | bytes 688136 | tf_op jit(solution)/shard_map/ppermute | solution.py:58
  104.1 12.8 %collective-permute-start.25 = (s16[2,112,512]{2,1,0:T(8,128)(2,1)S(1)}, s16[2,112,512]{2,1,0:T(8,128)(2,1)S(1)}, u32[]{:S(2)}, u32[]{:S(2)}) collective-permute-start(s16[2,112,512]{2,1,0:T(8,128)(2,1)S(1)} %copy-done.7), channel_id=1, source_target_pairs={{0,64},{32,96},{64,0},{96,32},{1,65},{33,97},{65,1},{97,33},{2,66}... | collective-permute-start | bytes 688136 | tf_op jit(solution)/shard_map/ppermute | solution.py:58
  104.2 19.5 %collective-permute-start.26 = (s16[2,112,512]{2,1,0:T(8,128)(2,1)S(1)}, s16[2,112,512]{2,1,0:T(8,128)(2,1)S(1)}, u32[]{:S(2)}, u32[]{:S(2)}) collective-permute-start(s16[2,112,512]{2,1,0:T(8,128)(2,1)S(1)} %copy-done.5), channel_id=1, source_target_pairs={{0,96},{32,0},{64,32},{96,64},{1,97},{33,1},{65,33},{97,65},{2,98}... | collective-permute-start | bytes 688136 | tf_op jit(solution)/shard_map/ppermute | solution.py:58
  106.0 18.1 %collective-permute-start.21 = (s16[2,88,512]{2,1,0:T(8,128)(2,1)S(1)}, s16[2,88,512]{2,1,0:T(8,128)(2,1)S(1)}, u32[]{:S(2)}, u32[]{:S(2)}) collective-permute-start(s16[2,88,512]{2,1,0:T(8,128)(2,1)S(1)} %get-tuple-element.61), channel_id=1, source_target_pairs={{0,32},{32,64},{64,96},{96,0},{1,33},{33,65},{65,97},{97,1},{2,34}... | collective-permute-start | bytes 540680 | tf_op jit(solution)/shard_map/ppermute | solution.py:58
  106.0 19.6 %collective-permute-start.22 = (s16[2,88,512]{2,1,0:T(8,128)(2,1)S(1)}, s16[2,88,512]{2,1,0:T(8,128)(2,1)S(1)}, u32[]{:S(2)}, u32[]{:S(2)}) collective-permute-start(s16[2,88,512]{2,1,0:T(8,128)(2,1)S(1)} %get-tuple-element.62), channel_id=1, source_target_pairs={{0,64},{32,96},{64,0},{96,32},{1,65},{33,97},{65,1},{97,33},{2,66}... | collective-permute-start | bytes 540680 | tf_op jit(solution)/shard_map/ppermute | solution.py:58
  108.6 18.9 %collective-permute-start.23 = (s16[2,88,512]{2,1,0:T(8,128)(2,1)S(1)}, s16[2,88,512]{2,1,0:T(8,128)(2,1)S(1)}, u32[]{:S(2)}, u32[]{:S(2)}) collective-permute-start(s16[2,88,512]{2,1,0:T(8,128)(2,1)S(1)} %get-tuple-element.63), channel_id=1, source_target_pairs={{0,96},{32,0},{64,32},{96,64},{1,97},{33,1},{65,33},{97,65},{2,98}... | collective-permute-start | bytes 540680 | tf_op jit(solution)/shard_map/ppermute | solution.py:58
  116.8 11.7 %collective-permute-start.30 = (bf16[112,500]{1,0:T(8,128)(2,1)S(1)}, bf16[112,500]{1,0:T(8,128)(2,1)S(1)}, u32[]{:S(2)}, u32[]{:S(2)}) collective-permute-start(bf16[112,500]{1,0:T(8,128)(2,1)S(1)} %get-tuple-element.75), channel_id=1, source_target_pairs={{0,1},{1,0},{2,3},{3,2},{4,5},{5,4},{6,7},{7,6},{8,9},{9,8},{10,11... | collective-permute-start | bytes 336008 | tf_op jit(solution)/shard_map/ppermute | solution.py:54
  (37 other events, 282.0 us)

commit v3 on v2

--- a/solution.py
+++ b/solution.py
@@ -80,32 +80,28 @@
 ):
     _, reps, rows, cols = acc.shape
     depth, width = w_own.shape[1:]
+    chips = t_buf.shape[0]
     block = table[16] * 2 + h
-    groups = [(0, 2), (2, 4), (4, 8), (8, 12), (12, 16)]
     over = 2 * SHARD - chip_cols
-    edges = [0] + [-(-(chip_cols * low + over) // 16) * 16 for low, _ in groups[1:]] + [depth]
-    t_refs = (t0, t1, t2, t3)
+    edges = [0] + [-(-(chip_cols * SIDE * g + over) // 16) * 16 for g in range(1, SIDE)] + [depth]
     w_copies = []
-    for g, (low, high) in enumerate(groups):
-        for chip in range(low, high):
-            place = table[21 + chip]
-            j, i = place // SIDE, place % SIDE
-            for arrival, t_ref in enumerate(t_refs):
-
-                @pl.when(j == arrival)
-                def _():
-                    pltpu.make_async_copy(t_ref.at[i], t_buf.at[chip], t_sem.at[chip]).start()
-
+    for g in range(SIDE):
         span = pl.ds(edges[g], edges[g + 1] - edges[g])
         for side, w in enumerate((w_own, w_other)):
-            copy = pltpu.make_async_copy(w.at[block, span], w_buf.at[side, span], w_sem.at[g, side])
-            copy.start()
-            w_copies.append(copy)
+            w_copies.append(pltpu.make_async_copy(w.at[block, span], w_buf.at[side, span], w_sem.at[g, side]))
+    for copy in w_copies[:2]:
+        copy.start()
+    for j, t_ref in enumerate((t0, t1, t2, t3)):
+        for i in range(SIDE):
+            chip = table[j * SIDE + i]
+            pltpu.make_async_copy(t_ref.at[i], t_buf.at[chip], t_sem.at[chip]).start()
+    for copy in w_copies[2:]:
+        copy.start()
     tail = w_buf.shape[1] - depth
     for side in range(2):
         w_buf[side, depth:, :] = jnp.zeros((tail, width), w_buf.dtype)
-    for g, (low, high) in enumerate(groups):
-        group = range(low, high)
+    for g in range(SIDE):
+        group = range(g * SIDE, (g + 1) * SIDE)
         for copy in w_copies[2 * g : 2 * g + 2]:
             copy.wait()
         for chip in group:
@@ -142,7 +138,7 @@
                 pltpu.VMEM((2, depth + 16, width), jnp.bfloat16),
                 pltpu.VMEM((2, SIDE, rows, COLS), jnp.float32),
                 pltpu.SemaphoreType.DMA((chips,)),
-                pltpu.SemaphoreType.DMA((5, 2)),
+                pltpu.SemaphoreType.DMA((SIDE, 2)),
             ],
         ),
         out_shape=[jax.ShapeDtypeStruct(code_shape, jnp.float32)] + [jax.ShapeDtypeStruct(code_shape, jnp.int16)] * 3,
@@ -205,17 +201,6 @@
     return jnp.stack([energy_j, energy_b], axis=1)
 
 
-def place_of(core, y, x):
-    chip = jnp.arange(SIDE * SIDE, dtype=jnp.int32)
-    hop_y, hop_x = jnp.mod(chip // SIDE - y, SIDE), jnp.mod(chip % SIDE - x, SIDE)
-
-    def slot(hop):
-        return jnp.where(hop == 0, 0, jnp.where(hop == 1, 2, jnp.where(hop == 2, 3, 1)))
-
-    first, second = jnp.where(core == 0, hop_x, hop_y), jnp.where(core == 0, hop_y, hop_x)
-    return slot(second) * SIDE + slot(first)
-
-
 def shards(amplitudes, block_table, intermediate, slab_energy, slab_irrep, occ_energy, virt_energy):
     blocks, slab, virt, shard = amplitudes.shape
     width = intermediate.shape[2]
@@ -242,7 +227,7 @@
     y_chip = jnp.where(core == 0, near[1], near[0])
     chips = jnp.mod(y + y_chip, SIDE) * SIDE + jnp.mod(x + x_chip, SIDE)
     table = jnp.concatenate(
-        [chips.reshape(-1), core[None], jnp.mod(rep + jnp.arange(SIDE, dtype=jnp.int32), SIDE), place_of(core, y, x)]
+        [chips.reshape(-1), core[None], jnp.mod(rep + jnp.arange(SIDE, dtype=jnp.int32), SIDE)]
     ).astype(jnp.int32)
 
     my_h = core * mine + jnp.arange(mine, dtype=jnp.int32)

time: 140 us -> 140 us (level)
  local copies, waits for them, and re-layouts: 11.2 us -> 8.5 us
  Pallas kernels: 31.2 us -> 33.7 us
  starting transfers between devices: 48.1 us -> 46.4 us
    pallas_call x4, Pallas kernels: 30 us -> 32.6 us  [multiply(): pl.pallas_call(functools.partial(product_kernel, h, chip_cols), grid_spec...]
    slice x1, local copies, waits for them, and re-layouts: 1.96 us -> 0.08 us  [build(): node('both0')[k]]
    ppermute x6, starting transfers between devices: 10.8 us -> 9.24 us  [swap_cores(): lax.ppermute(value, 'con', [(i, i ^ 1) for i in range(2 * SIDE * SIDE)])]
    slice x1, local copies, waits for them, and re-layouts: 1.49 us -> 0.08 us  [build(): node('both1')[k]]
    unnamed x64 -> x60, local copies, waits for them, and re-layouts: 4.25 us -> 4.82 us
  transfers between devices with their start and end apart: 34 -> 34, of which waited for: 9 -> 10; matrix products, arithmetic and copies ran while one was open for 7% -> 5% of each run, Pallas kernels for 22% -> 24%
where the time goes in v3:
time: 140 us; the launch traced here: 139 us
  starting transfers between devices  46.4 us (33%)
  waiting for transfers between devices  42.7 us (30%)
  Pallas kernels  33.7 us (24%)
  local copies, waits for them, and re-layouts  8.5 us (6%)
  other arithmetic  7.36 us (5%)
    ppermute x16, waiting for transfers between devices, ring(): return lax.ppermute(value, 'con', ring_pairs(stage, hop))  33.4 us
    pallas_call x4, Pallas kernels, multiply(): pl.pallas_call(functools.partial(product_kernel, h, chip_cols), grid_spec...  32.6 us
    ppermute x16, starting transfers between devices, ring(): return lax.ppermute(value, 'con', ring_pairs(stage, hop))  21.5 us
    ppermute x12, starting transfers between devices, to_replica(): lax.ppermute(value, 'rep', [(i, (i + hop) % SIDE) for i in range(SIDE)])  15.7 us
    ppermute x6, starting transfers between devices, swap_cores(): lax.ppermute(value, 'con', [(i, i ^ 1) for i in range(2 * SIDE * SIDE)])  9.24 us
    ppermute x12, waiting for transfers between devices, to_replica(): lax.ppermute(value, 'rep', [(i, (i + hop) % SIDE) for i in range(SIDE)])  5.75 us
    unnamed x60, local copies, waits for them, and re-layouts  4.82 us
    ppermute x6, waiting for transfers between devices, swap_cores(): lax.ppermute(value, 'con', [(i, i ^ 1) for i in range(2 * SIDE * SIDE)])  3.56 us
  transfers between devices with their start and end apart: 34, of which 10 were waited for; matrix products, arithmetic and copies ran while one was open for 5% of the time, Pallas kernels for 24%

profile of v3, /device:TPU:1, one launch (start us, length us, event | category | flops | bytes accessed | tf_op | source)
XLA Modules:
  0.0 139.3 jit_solution(2215328031233163407)
XLA Ops:
  10.0 9.7 %collective-permute-done.1 = bf16[2,800,256]{2,1,0:T(8,128)(2,1)S(1)} collective-permute-done((bf16[2,800,256]{2,1,0:T(8,128)(2,1)S(1)}, bf16[2,800,256]{2,1,0:T(8,128)(2,1)S(1)}, u32[]{:S(2)}, u32[]{:S(2)}) %collective-permute-start.1) | collective-permute-done | bytes 819232 | tf_op jit(solution)/shard_map/ppermute | solution.py:50
  20.1 2.7 %collective-permute-start.8 = (bf16[800,256]{1,0:T(8,128)(2,1)S(1)}, bf16[800,256]{1,0:T(8,128)(2,1)S(1)}, u32[]{:S(2)}, u32[]{:S(2)}) collective-permute-start(bf16[800,256]{1,0:T(8,128)(2,1)S(1)} %get-tuple-element.89), channel_id=1, source_target_pairs={{0,6},{1,25},{2,0},{3,27},{4,2},{5,29},{6,4},{7,31},{8,14},{9,1},{... | collective-permute-start | bytes 1228808 | tf_op jit(solution)/shard_map/ppermute | solution.py:50
  23.0 5.1 %collective-permute-done.3 = bf16[800,256]{1,0:T(8,128)(2,1)S(1)} collective-permute-done((bf16[800,256]{1,0:T(8,128)(2,1)S(1)}, bf16[800,256]{1,0:T(8,128)(2,1)S(1)}, u32[]{:S(2)}, u32[]{:S(2)}) %collective-permute-start.3) | collective-permute-done | bytes 409632 | tf_op jit(solution)/shard_map/ppermute | solution.py:50
  29.7 2.1 %collective-permute-start.5 = (bf16[4,448,256]{2,1,0:T(8,128)(2,1)S(1)}, bf16[4,448,256]{2,1,0:T(8,128)(2,1)}, u32[]{:S(2)}, u32[]{:S(2)}) collective-permute-start(bf16[4,448,256]{2,1,0:T(8,128)(2,1)S(1)} %bitcast.34), channel_id=1, source_target_pairs={{0,24},{1,7},{2,26},{3,1},{4,28},{5,3},{6,30},{7,5},{8,0},{9,15},{... | collective-permute-start | bytes 2752520 | tf_op jit(solution)/shard_map/ppermute | solution.py:50
  35.4 7.5 %collective-permute-done.4.t1 = bf16[4,448,256]{2,1,0:T(8,128)(2,1)} collective-permute-done((bf16[4,448,256]{2,1,0:T(8,128)(2,1)S(1)}, bf16[4,448,256]{2,1,0:T(8,128)(2,1)}, u32[]{:S(2)}, u32[]{:S(2)}) %collective-permute-start.4) | collective-permute-done | bytes 917536 | tf_op jit(solution)/shard_map/ppermute | solution.py:50
  43.0 9.2 %collective-permute-done.10.t2 = bf16[4,448,256]{2,1,0:T(8,128)(2,1)} collective-permute-done((bf16[4,448,256]{2,1,0:T(8,128)(2,1)S(1)}, bf16[4,448,256]{2,1,0:T(8,128)(2,1)}, u32[]{:S(2)}, u32[]{:S(2)}) %collective-permute-start.10) | collective-permute-done | bytes 917536 | tf_op jit(solution)/shard_map/ppermute | solution.py:50
  52.1 3.2 %collective-permute-start.11 = (bf16[4,448,256]{2,1,0:T(8,128)(2,1)}, bf16[4,448,256]{2,1,0:T(8,128)(2,1)S(1)}, u32[]{:S(2)}, u32[]{:S(2)}) collective-permute-start(bf16[4,448,256]{2,1,0:T(8,128)(2,1)} %collective-permute-done.10.t2), channel_id=1, source_target_pairs={{0,24},{1,7},{2,26},{3,1},{4,28},{5,3},{6,30},{7,5},{8,0},{9,15},{... | collective-permute-start | bytes 2752520 | tf_op jit(solution)/shard_map/ppermute | solution.py:50
  57.8 2.7 %collective-permute-start.16 = (bf16[4,352,256]{2,1,0:T(8,128)(2,1)S(1)}, bf16[4,352,256]{2,1,0:T(8,128)(2,1)}, u32[]{:S(2)}, u32[]{:S(2)}) collective-permute-start(bf16[4,352,256]{2,1,0:T(8,128)(2,1)S(1)} %bitcast.39), channel_id=1, source_target_pairs={{0,24},{1,7},{2,26},{3,1},{4,28},{5,3},{6,30},{7,5},{8,0},{9,15},{... | collective-permute-start | bytes 2162696 | tf_op jit(solution)/shard_map/ppermute | solution.py:50
  60.6 1.9 %collective-permute-done.6.t3 = bf16[4,448,256]{2,1,0:T(8,128)(2,1)S(1)} collective-permute-done((bf16[4,448,256]{2,1,0:T(8,128)(2,1)}, bf16[4,448,256]{2,1,0:T(8,128)(2,1)S(1)}, u32[]{:S(2)}, u32[]{:S(2)}) %collective-permute-start.6) | collective-permute-done | bytes 917536 | tf_op jit(solution)/shard_map/ppermute | solution.py:50
  62.5 2.7 %collective-permute-start.13 = (bf16[4,352,256]{2,1,0:T(8,128)(2,1)S(1)}, bf16[4,352,256]{2,1,0:T(8,128)(2,1)}, u32[]{:S(2)}, u32[]{:S(2)}) collective-permute-start(bf16[4,352,256]{2,1,0:T(8,128)(2,1)S(1)} %bitcast.43), channel_id=1, source_target_pairs={{0,24},{1,7},{2,26},{3,1},{4,28},{5,3},{6,30},{7,5},{8,0},{9,15},{... | collective-permute-start | bytes 2162696 | tf_op jit(solution)/shard_map/ppermute | solution.py:50
  65.1 8.5 %shard_map.91 = (f32[2,112,512]{2,1,0:T(8,128)S(1)}, s16[2,112,512]{2,1,0:T(8,128)(2,1)S(1)}, s16[2,112,512]{2,1,0:T(8,128)(2,1)S(1)}, s16[2,112,512]{2,1,0:T(8,128)(2,1)S(1)}) custom-call(s32[21]{0:T(128)S(1)} %pad_add_fusion.table, bf16[4,448,256]{2,1,0:T(8,128)(2,1)S(1)} %bitcast.35, bf16[4,448,256]{2,1,0:T(8,128)(2,1)} %collective-permute-done.4.t1, ...), custom_call_target="tpu_custom_call" | custom-call | flops 3584000000 | bytes 24000000 | tf_op jit(solution)/shard_map/pallas_call | solution.py:129
  74.4 1.6 %collective-permute-start.17 = (s16[2,112,512]{2,1,0:T(8,128)(2,1)S(1)}, s16[2,112,512]{2,1,0:T(8,128)(2,1)S(1)}, u32[]{:S(2)}, u32[]{:S(2)}) collective-permute-start(s16[2,112,512]{2,1,0:T(8,128)(2,1)S(1)} %get-tuple-element.53), channel_id=1, source_target_pairs={{0,32},{32,64},{64,96},{96,0},{1,33},{33,65},{65,97},{97,1},{2,34}... | collective-permute-start | bytes 688136 | tf_op jit(solution)/shard_map/ppermute | solution.py:58
  76.1 8.5 %shard_map.92 = (f32[2,112,512]{2,1,0:T(8,128)S(1)}, s16[2,112,512]{2,1,0:T(8,128)(2,1)S(1)}, s16[2,112,512]{2,1,0:T(8,128)(2,1)S(1)}, s16[2,112,512]{2,1,0:T(8,128)(2,1)S(1)}) custom-call(s32[21]{0:T(128)S(1)} %pad_add_fusion.table, bf16[4,448,256]{2,1,0:T(8,128)(2,1)S(1)} %bitcast.38, bf16[4,448,256]{2,1,0:T(8,128)(2,1)} %collective-permute-done.9.t1, ...), custom_call_target="tpu_custom_call" | custom-call | flops 3584000000 | bytes 24000000 | tf_op jit(solution)/shard_map/pallas_call | solution.py:129
  87.5 2.7 %collective-permute-start.18 = (bf16[4,352,256]{2,1,0:T(8,128)(2,1)}, bf16[4,352,256]{2,1,0:T(8,128)(2,1)S(1)}, u32[]{:S(2)}, u32[]{:S(2)}) collective-permute-start(bf16[4,352,256]{2,1,0:T(8,128)(2,1)} %collective-permute-done.16.t2), channel_id=1, source_target_pairs={{0,24},{1,7},{2,26},{3,1},{4,28},{5,3},{6,30},{7,5},{8,0},{9,15},{... | collective-permute-start | bytes 2162696 | tf_op jit(solution)/shard_map/ppermute | solution.py:50
  91.0 1.7 %collective-permute-start.24 = (s16[2,112,512]{2,1,0:T(8,128)(2,1)}, s16[2,112,512]{2,1,0:T(8,128)(2,1)S(1)}, u32[]{:S(2)}, u32[]{:S(2)}) collective-permute-start(s16[2,112,512]{2,1,0:T(8,128)(2,1)} %copy-done.9), channel_id=1, source_target_pairs={{0,32},{32,64},{64,96},{96,0},{1,33},{33,65},{65,97},{97,1},{2,34}... | collective-permute-start | bytes 688136 | tf_op jit(solution)/shard_map/ppermute | solution.py:58
  92.7 1.8 %collective-permute-start.19 = (s16[2,112,512]{2,1,0:T(8,128)(2,1)}, s16[2,112,512]{2,1,0:T(8,128)(2,1)S(1)}, u32[]{:S(2)}, u32[]{:S(2)}) collective-permute-start(s16[2,112,512]{2,1,0:T(8,128)(2,1)} %copy-done.8), channel_id=1, source_target_pairs={{0,64},{32,96},{64,0},{96,32},{1,65},{33,97},{65,1},{97,33},{2,66}... | collective-permute-start | bytes 688136 | tf_op jit(solution)/shard_map/ppermute | solution.py:58
  94.5 2.0 %collective-permute-start.20 = (s16[2,112,512]{2,1,0:T(8,128)(2,1)S(1)}, s16[2,112,512]{2,1,0:T(8,128)(2,1)S(1)}, u32[]{:S(2)}, u32[]{:S(2)}) collective-permute-start(s16[2,112,512]{2,1,0:T(8,128)(2,1)S(1)} %get-tuple-element.58), channel_id=1, source_target_pairs={{0,96},{32,0},{64,32},{96,64},{1,97},{33,1},{65,33},{97,65},{2,98}... | collective-permute-start | bytes 688136 | tf_op jit(solution)/shard_map/ppermute | solution.py:58
  96.4 8.1 %shard_map.93 = (f32[2,88,512]{2,1,0:T(8,128)S(1)}, s16[2,88,512]{2,1,0:T(8,128)(2,1)S(1)}, s16[2,88,512]{2,1,0:T(8,128)(2,1)S(1)}, s16[2,88,512]{2,1,0:T(8,128)(2,1)S(1)}) custom-call(s32[21]{0:T(128)S(1)} %pad_add_fusion.table, bf16[4,352,256]{2,1,0:T(8,128)(2,1)S(1)} %bitcast.44, bf16[4,352,256]{2,1,0:T(8,128)(2,1)} %collective-permute-done.12.t1, ...), custom_call_target="tpu_custom_call" | custom-call | flops 2816000000 | bytes 24000000 | tf_op jit(solution)/shard_map/pallas_call | solution.py:129
  104.7 1.9 %collective-permute-start.26 = (s16[2,112,512]{2,1,0:T(8,128)(2,1)S(1)}, s16[2,112,512]{2,1,0:T(8,128)(2,1)S(1)}, u32[]{:S(2)}, u32[]{:S(2)}) collective-permute-start(s16[2,112,512]{2,1,0:T(8,128)(2,1)S(1)} %copy-done.5), channel_id=1, source_target_pairs={{0,96},{32,0},{64,32},{96,64},{1,97},{33,1},{65,33},{97,65},{2,98}... | collective-permute-start | bytes 688136 | tf_op jit(solution)/shard_map/ppermute | solution.py:58
  106.6 2.5 %collective-permute-start.22 = (s16[2,88,512]{2,1,0:T(8,128)(2,1)S(1)}, s16[2,88,512]{2,1,0:T(8,128)(2,1)S(1)}, u32[]{:S(2)}, u32[]{:S(2)}) collective-permute-start(s16[2,88,512]{2,1,0:T(8,128)(2,1)S(1)} %get-tuple-element.62), channel_id=1, source_target_pairs={{0,64},{32,96},{64,0},{96,32},{1,65},{33,97},{65,1},{97,33},{2,66}... | collective-permute-start | bytes 540680 | tf_op jit(solution)/shard_map/ppermute | solution.py:58
  109.8 7.4 %shard_map.94 = (f32[2,88,512]{2,1,0:T(8,128)S(1)}, s16[2,88,512]{2,1,0:T(8,128)(2,1)S(1)}, s16[2,88,512]{2,1,0:T(8,128)(2,1)S(1)}, s16[2,88,512]{2,1,0:T(8,128)(2,1)S(1)}) custom-call(s32[21]{0:T(128)S(1)} %pad_add_fusion.table, bf16[4,352,256]{2,1,0:T(8,128)(2,1)S(1)} %bitcast.41, bf16[4,352,256]{2,1,0:T(8,128)(2,1)} %collective-permute-done.15.t1, ...), custom_call_target="tpu_custom_call" | custom-call | flops 2816000000 | bytes 24000000 | tf_op jit(solution)/shard_map/pallas_call | solution.py:129
  117.5 5.2 %collective-permute-start.30 = (bf16[112,500]{1,0:T(8,128)(2,1)S(1)}, bf16[112,500]{1,0:T(8,128)(2,1)S(1)}, u32[]{:S(2)}, u32[]{:S(2)}) collective-permute-start(bf16[112,500]{1,0:T(8,128)(2,1)S(1)} %get-tuple-element.75), channel_id=1, source_target_pairs={{0,1},{1,0},{2,3},{3,2},{4,5},{5,4},{6,7},{7,6},{8,9},{9,8},{10,11... | collective-permute-start | bytes 336008 | tf_op jit(solution)/shard_map/ppermute | solution.py:54
  124.8 1.8 %collective-permute-start.28 = (s16[2,88,512]{2,1,0:T(8,128)(2,1)S(1)}, s16[2,88,512]{2,1,0:T(8,128)(2,1)S(1)}, u32[]{:S(2)}, u32[]{:S(2)}) collective-permute-start(s16[2,88,512]{2,1,0:T(8,128)(2,1)S(1)} %get-tuple-element.71), channel_id=1, source_target_pairs={{0,64},{32,96},{64,0},{96,32},{1,65},{33,97},{65,1},{97,33},{2,66}... | collective-permute-start | bytes 540680 | tf_op jit(solution)/shard_map/ppermute | solution.py:58
  130.4 4.5 %collective-permute-done.28.code2 = s16[2,88,512]{2,1,0:T(8,128)(2,1)S(1)} collective-permute-done((s16[2,88,512]{2,1,0:T(8,128)(2,1)S(1)}, s16[2,88,512]{2,1,0:T(8,128)(2,1)S(1)}, u32[]{:S(2)}, u32[]{:S(2)}) %collective-permute-start.28) | collective-permute-done | bytes 180256 | tf_op jit(solution)/shard_map/ppermute | solution.py:58
  (168 shorter events, 33.7 us)
Async XLA Ops:
  5.5 56.9 %collective-permute-start.7 = (bf16[4,4000,500]{2,1,0:T(8,128)(2,1)}, bf16[4,4000,500]{2,1,0:T(8,128)(2,1)}, u32[]{:S(2)}, u32[]{:S(2)}) collective-permute-start(bf16[4,4000,500]{2,1,0:T(8,128)(2,1)} %w_own.3), channel_id=1, source_target_pairs={{0,1},{1,0},{2,3},{3,2},{4,5},{5,4},{6,7},{7,6},{8,9},{9,8},{10,11... | collective-permute-start | bytes 48000008 | tf_op jit(solution)/shard_map/ppermute | solution.py:54
  6.8 12.9 %collective-permute-start.1 = (bf16[2,800,256]{2,1,0:T(8,128)(2,1)S(1)}, bf16[2,800,256]{2,1,0:T(8,128)(2,1)S(1)}, u32[]{:S(2)}, u32[]{:S(2)}) collective-permute-start(bf16[2,800,256]{2,1,0:T(8,128)(2,1)S(1)} %pad.4), channel_id=1, source_target_pairs={{0,2},{1,9},{2,4},{3,11},{4,6},{5,13},{6,0},{7,15},{8,10},{9,17},{... | collective-permute-start | bytes 2457608 | tf_op jit(solution)/shard_map/ppermute | solution.py:50
  8.4 11.7 %collective-permute-start.2 = (bf16[2,800,256]{2,1,0:T(8,128)(2,1)S(1)}, bf16[2,800,256]{2,1,0:T(8,128)(2,1)S(1)}, u32[]{:S(2)}, u32[]{:S(2)}) collective-permute-start(bf16[2,800,256]{2,1,0:T(8,128)(2,1)S(1)} %pad.4), channel_id=1, source_target_pairs={{0,6},{1,25},{2,0},{3,27},{4,2},{5,29},{6,4},{7,31},{8,14},{9,1},{... | collective-permute-start | bytes 2457608 | tf_op jit(solution)/shard_map/ppermute | solution.py:50
  29.0 13.9 %collective-permute-start.4 = (bf16[4,448,256]{2,1,0:T(8,128)(2,1)S(1)}, bf16[4,448,256]{2,1,0:T(8,128)(2,1)}, u32[]{:S(2)}, u32[]{:S(2)}) collective-permute-start(bf16[4,448,256]{2,1,0:T(8,128)(2,1)S(1)} %bitcast.33), channel_id=1, source_target_pairs={{0,8},{1,3},{2,10},{3,5},{4,12},{5,7},{6,14},{7,1},{8,16},{9,11},{... | collective-permute-start | bytes 2752520 | tf_op jit(solution)/shard_map/ppermute | solution.py:50
  29.7 26.8 %collective-permute-start.5 = (bf16[4,448,256]{2,1,0:T(8,128)(2,1)S(1)}, bf16[4,448,256]{2,1,0:T(8,128)(2,1)}, u32[]{:S(2)}, u32[]{:S(2)}) collective-permute-start(bf16[4,448,256]{2,1,0:T(8,128)(2,1)S(1)} %bitcast.34), channel_id=1, source_target_pairs={{0,24},{1,7},{2,26},{3,1},{4,28},{5,3},{6,30},{7,5},{8,0},{9,15},{... | collective-permute-start | bytes 2752520 | tf_op jit(solution)/shard_map/ppermute | solution.py:50
  32.6 19.6 %collective-permute-start.10 = (bf16[4,448,256]{2,1,0:T(8,128)(2,1)S(1)}, bf16[4,448,256]{2,1,0:T(8,128)(2,1)}, u32[]{:S(2)}, u32[]{:S(2)}) collective-permute-start(bf16[4,448,256]{2,1,0:T(8,128)(2,1)S(1)} %bitcast.36), channel_id=1, source_target_pairs={{0,24},{1,7},{2,26},{3,1},{4,28},{5,3},{6,30},{7,5},{8,0},{9,15},{... | collective-permute-start | bytes 2752520 | tf_op jit(solution)/shard_map/ppermute | solution.py:50
  34.9 22.8 %collective-permute-start.9 = (bf16[4,448,256]{2,1,0:T(8,128)(2,1)S(1)}, bf16[4,448,256]{2,1,0:T(8,128)(2,1)}, u32[]{:S(2)}, u32[]{:S(2)}) collective-permute-start(bf16[4,448,256]{2,1,0:T(8,128)(2,1)S(1)} %bitcast.37), channel_id=1, source_target_pairs={{0,8},{1,3},{2,10},{3,5},{4,12},{5,7},{6,14},{7,1},{8,16},{9,11},{... | collective-permute-start | bytes 2752520 | tf_op jit(solution)/shard_map/ppermute | solution.py:50
  42.9 19.6 %collective-permute-start.6 = (bf16[4,448,256]{2,1,0:T(8,128)(2,1)}, bf16[4,448,256]{2,1,0:T(8,128)(2,1)S(1)}, u32[]{:S(2)}, u32[]{:S(2)}) collective-permute-start(bf16[4,448,256]{2,1,0:T(8,128)(2,1)} %collective-permute-done.4.t1), channel_id=1, source_target_pairs={{0,8},{1,3},{2,10},{3,5},{4,12},{5,7},{6,14},{7,1},{8,16},{9,11},{... | collective-permute-start | bytes 2752520 | tf_op jit(solution)/shard_map/ppermute | solution.py:50
  52.1 23.9 %collective-permute-start.11 = (bf16[4,448,256]{2,1,0:T(8,128)(2,1)}, bf16[4,448,256]{2,1,0:T(8,128)(2,1)S(1)}, u32[]{:S(2)}, u32[]{:S(2)}) collective-permute-start(bf16[4,448,256]{2,1,0:T(8,128)(2,1)} %collective-permute-done.10.t2), channel_id=1, source_target_pairs={{0,24},{1,7},{2,26},{3,1},{4,28},{5,3},{6,30},{7,5},{8,0},{9,15},{... | collective-permute-start | bytes 2752520 | tf_op jit(solution)/shard_map/ppermute | solution.py:50
  56.5 18.0 %collective-permute-start.12 = (bf16[4,352,256]{2,1,0:T(8,128)(2,1)S(1)}, bf16[4,352,256]{2,1,0:T(8,128)(2,1)}, u32[]{:S(2)}, u32[]{:S(2)}) collective-permute-start(bf16[4,352,256]{2,1,0:T(8,128)(2,1)S(1)} %bitcast.42), channel_id=1, source_target_pairs={{0,8},{1,3},{2,10},{3,5},{4,12},{5,7},{6,14},{7,1},{8,16},{9,11},{... | collective-permute-start | bytes 2162696 | tf_op jit(solution)/shard_map/ppermute | solution.py:50
  57.8 29.7 %collective-permute-start.16 = (bf16[4,352,256]{2,1,0:T(8,128)(2,1)S(1)}, bf16[4,352,256]{2,1,0:T(8,128)(2,1)}, u32[]{:S(2)}, u32[]{:S(2)}) collective-permute-start(bf16[4,352,256]{2,1,0:T(8,128)(2,1)S(1)} %bitcast.39), channel_id=1, source_target_pairs={{0,24},{1,7},{2,26},{3,1},{4,28},{5,3},{6,30},{7,5},{8,0},{9,15},{... | collective-permute-start | bytes 2162696 | tf_op jit(solution)/shard_map/ppermute | solution.py:50
  62.5 42.1 %collective-permute-start.15 = (bf16[4,352,256]{2,1,0:T(8,128)(2,1)S(1)}, bf16[4,352,256]{2,1,0:T(8,128)(2,1)}, u32[]{:S(2)}, u32[]{:S(2)}) collective-permute-start(bf16[4,352,256]{2,1,0:T(8,128)(2,1)S(1)} %bitcast.40), channel_id=1, source_target_pairs={{0,8},{1,3},{2,10},{3,5},{4,12},{5,7},{6,14},{7,1},{8,16},{9,11},{... | collective-permute-start | bytes 2162696 | tf_op jit(solution)/shard_map/ppermute | solution.py:50
  62.5 30.2 %collective-permute-start.13 = (bf16[4,352,256]{2,1,0:T(8,128)(2,1)S(1)}, bf16[4,352,256]{2,1,0:T(8,128)(2,1)}, u32[]{:S(2)}, u32[]{:S(2)}) collective-permute-start(bf16[4,352,256]{2,1,0:T(8,128)(2,1)S(1)} %bitcast.43), channel_id=1, source_target_pairs={{0,24},{1,7},{2,26},{3,1},{4,28},{5,3},{6,30},{7,5},{8,0},{9,15},{... | collective-permute-start | bytes 2162696 | tf_op jit(solution)/shard_map/ppermute | solution.py:50
  74.4 13.0 %collective-permute-start.17 = (s16[2,112,512]{2,1,0:T(8,128)(2,1)S(1)}, s16[2,112,512]{2,1,0:T(8,128)(2,1)S(1)}, u32[]{:S(2)}, u32[]{:S(2)}) collective-permute-start(s16[2,112,512]{2,1,0:T(8,128)(2,1)S(1)} %get-tuple-element.53), channel_id=1, source_target_pairs={{0,32},{32,64},{64,96},{96,0},{1,33},{33,65},{65,97},{97,1},{2,34}... | collective-permute-start | bytes 688136 | tf_op jit(solution)/shard_map/ppermute | solution.py:58
  76.1 18.4 %collective-permute-start.14 = (bf16[4,352,256]{2,1,0:T(8,128)(2,1)}, bf16[4,352,256]{2,1,0:T(8,128)(2,1)}, u32[]{:S(2)}, u32[]{:S(2)}) collective-permute-start(bf16[4,352,256]{2,1,0:T(8,128)(2,1)} %collective-permute-done.12.t1), channel_id=1, source_target_pairs={{0,8},{1,3},{2,10},{3,5},{4,12},{5,7},{6,14},{7,1},{8,16},{9,11},{... | collective-permute-start | bytes 2162696 | tf_op jit(solution)/shard_map/ppermute | solution.py:50
  87.5 21.6 %collective-permute-start.18 = (bf16[4,352,256]{2,1,0:T(8,128)(2,1)}, bf16[4,352,256]{2,1,0:T(8,128)(2,1)S(1)}, u32[]{:S(2)}, u32[]{:S(2)}) collective-permute-start(bf16[4,352,256]{2,1,0:T(8,128)(2,1)} %collective-permute-done.16.t2), channel_id=1, source_target_pairs={{0,24},{1,7},{2,26},{3,1},{4,28},{5,3},{6,30},{7,5},{8,0},{9,15},{... | collective-permute-start | bytes 2162696 | tf_op jit(solution)/shard_map/ppermute | solution.py:50
  91.0 13.7 %collective-permute-start.24 = (s16[2,112,512]{2,1,0:T(8,128)(2,1)}, s16[2,112,512]{2,1,0:T(8,128)(2,1)S(1)}, u32[]{:S(2)}, u32[]{:S(2)}) collective-permute-start(s16[2,112,512]{2,1,0:T(8,128)(2,1)} %copy-done.9), channel_id=1, source_target_pairs={{0,32},{32,64},{64,96},{96,0},{1,33},{33,65},{65,97},{97,1},{2,34}... | collective-permute-start | bytes 688136 | tf_op jit(solution)/shard_map/ppermute | solution.py:58
  92.7 13.9 %collective-permute-start.19 = (s16[2,112,512]{2,1,0:T(8,128)(2,1)}, s16[2,112,512]{2,1,0:T(8,128)(2,1)S(1)}, u32[]{:S(2)}, u32[]{:S(2)}) collective-permute-start(s16[2,112,512]{2,1,0:T(8,128)(2,1)} %copy-done.8), channel_id=1, source_target_pairs={{0,64},{32,96},{64,0},{96,32},{1,65},{33,97},{65,1},{97,33},{2,66}... | collective-permute-start | bytes 688136 | tf_op jit(solution)/shard_map/ppermute | solution.py:58
  94.5 12.1 %collective-permute-start.20 = (s16[2,112,512]{2,1,0:T(8,128)(2,1)S(1)}, s16[2,112,512]{2,1,0:T(8,128)(2,1)S(1)}, u32[]{:S(2)}, u32[]{:S(2)}) collective-permute-start(s16[2,112,512]{2,1,0:T(8,128)(2,1)S(1)} %get-tuple-element.58), channel_id=1, source_target_pairs={{0,96},{32,0},{64,32},{96,64},{1,97},{33,1},{65,33},{97,65},{2,98}... | collective-permute-start | bytes 688136 | tf_op jit(solution)/shard_map/ppermute | solution.py:58
  104.6 13.0 %collective-permute-start.25 = (s16[2,112,512]{2,1,0:T(8,128)(2,1)S(1)}, s16[2,112,512]{2,1,0:T(8,128)(2,1)S(1)}, u32[]{:S(2)}, u32[]{:S(2)}) collective-permute-start(s16[2,112,512]{2,1,0:T(8,128)(2,1)S(1)} %copy-done.7), channel_id=1, source_target_pairs={{0,64},{32,96},{64,0},{96,32},{1,65},{33,97},{65,1},{97,33},{2,66}... | collective-permute-start | bytes 688136 | tf_op jit(solution)/shard_map/ppermute | solution.py:58
  104.7 18.2 %collective-permute-start.26 = (s16[2,112,512]{2,1,0:T(8,128)(2,1)S(1)}, s16[2,112,512]{2,1,0:T(8,128)(2,1)S(1)}, u32[]{:S(2)}, u32[]{:S(2)}) collective-permute-start(s16[2,112,512]{2,1,0:T(8,128)(2,1)S(1)} %copy-done.5), channel_id=1, source_target_pairs={{0,96},{32,0},{64,32},{96,64},{1,97},{33,1},{65,33},{97,65},{2,98}... | collective-permute-start | bytes 688136 | tf_op jit(solution)/shard_map/ppermute | solution.py:58
  106.6 16.8 %collective-permute-start.21 = (s16[2,88,512]{2,1,0:T(8,128)(2,1)S(1)}, s16[2,88,512]{2,1,0:T(8,128)(2,1)S(1)}, u32[]{:S(2)}, u32[]{:S(2)}) collective-permute-start(s16[2,88,512]{2,1,0:T(8,128)(2,1)S(1)} %get-tuple-element.61), channel_id=1, source_target_pairs={{0,32},{32,64},{64,96},{96,0},{1,33},{33,65},{65,97},{97,1},{2,34}... | collective-permute-start | bytes 540680 | tf_op jit(solution)/shard_map/ppermute | solution.py:58
  106.6 18.3 %collective-permute-start.22 = (s16[2,88,512]{2,1,0:T(8,128)(2,1)S(1)}, s16[2,88,512]{2,1,0:T(8,128)(2,1)S(1)}, u32[]{:S(2)}, u32[]{:S(2)}) collective-permute-start(s16[2,88,512]{2,1,0:T(8,128)(2,1)S(1)} %get-tuple-element.62), channel_id=1, source_target_pairs={{0,64},{32,96},{64,0},{96,32},{1,65},{33,97},{65,1},{97,33},{2,66}... | collective-permute-start | bytes 540680 | tf_op jit(solution)/shard_map/ppermute | solution.py:58
  109.1 17.5 %collective-permute-start.23 = (s16[2,88,512]{2,1,0:T(8,128)(2,1)S(1)}, s16[2,88,512]{2,1,0:T(8,128)(2,1)S(1)}, u32[]{:S(2)}, u32[]{:S(2)}) collective-permute-start(s16[2,88,512]{2,1,0:T(8,128)(2,1)S(1)} %get-tuple-element.63), channel_id=1, source_target_pairs={{0,96},{32,0},{64,32},{96,64},{1,97},{33,1},{65,33},{97,65},{2,98}... | collective-permute-start | bytes 540680 | tf_op jit(solution)/shard_map/ppermute | solution.py:58
  (35 other events, 240.8 us)

commit v4 on v3

--- a/solution.py
+++ b/solution.py
@@ -83,9 +83,10 @@
     chips = t_buf.shape[0]
     block = table[16] * 2 + h
     over = 2 * SHARD - chip_cols
-    edges = [0] + [-(-(chip_cols * SIDE * g + over) // 16) * 16 for g in range(1, SIDE)] + [depth]
+    groups = ((0, 2), (2, 4), (4, 8), (8, 12), (12, 16))
+    edges = [0] + [-(-(chip_cols * low + over) // 16) * 16 for low, _ in groups[1:]] + [depth]
     w_copies = []
-    for g in range(SIDE):
+    for g in range(len(groups)):
         span = pl.ds(edges[g], edges[g + 1] - edges[g])
         for side, w in enumerate((w_own, w_other)):
             w_copies.append(pltpu.make_async_copy(w.at[block, span], w_buf.at[side, span], w_sem.at[g, side]))
@@ -100,8 +101,8 @@
     tail = w_buf.shape[1] - depth
     for side in range(2):
         w_buf[side, depth:, :] = jnp.zeros((tail, width), w_buf.dtype)
-    for g in range(SIDE):
-        group = range(g * SIDE, (g + 1) * SIDE)
+    for g, (low, high) in enumerate(groups):
+        group = range(low, high)
         for copy in w_copies[2 * g : 2 * g + 2]:
             copy.wait()
         for chip in group:
@@ -138,7 +139,7 @@
                 pltpu.VMEM((2, depth + 16, width), jnp.bfloat16),
                 pltpu.VMEM((2, SIDE, rows, COLS), jnp.float32),
                 pltpu.SemaphoreType.DMA((chips,)),
-                pltpu.SemaphoreType.DMA((SIDE, 2)),
+                pltpu.SemaphoreType.DMA((5, 2)),
             ],
         ),
         out_shape=[jax.ShapeDtypeStruct(code_shape, jnp.float32)] + [jax.ShapeDtypeStruct(code_shape, jnp.int16)] * 3,

time: 140 us -> 141 us (level)
  transfers between devices with their start and end apart: 34 -> 34, of which waited for: 10 -> 10; matrix products, arithmetic and copies ran while one was open for 5% -> 5% of each run, Pallas kernels for 24% -> 25%
where the time goes in v4:
time: 141 us
  starting transfers between devices  46.5 us (33%)
  waiting for transfers between devices  42.7 us (30%)
  Pallas kernels  34.9 us (25%)
  local copies, waits for them, and re-layouts  8.5 us (6%)
  other arithmetic  7.36 us (5%)
    pallas_call x4, Pallas kernels, multiply(): pl.pallas_call(functools.partial(product_kernel, h, chip_cols), grid_spec...  33.7 us
    ppermute x16, waiting for transfers between devices, ring(): return lax.ppermute(value, 'con', ring_pairs(stage, hop))  33.4 us
    ppermute x16, starting transfers between devices, ring(): return lax.ppermute(value, 'con', ring_pairs(stage, hop))  21.5 us
    ppermute x12, starting transfers between devices, to_replica(): lax.ppermute(value, 'rep', [(i, (i + hop) % SIDE) for i in range(SIDE)])  15.7 us
    ppermute x6, starting transfers between devices, swap_cores(): lax.ppermute(value, 'con', [(i, i ^ 1) for i in range(2 * SIDE * SIDE)])  9.34 us
    ppermute x12, waiting for transfers between devices, to_replica(): lax.ppermute(value, 'rep', [(i, (i + hop) % SIDE) for i in range(SIDE)])  5.75 us
    unnamed x60, local copies, waits for them, and re-layouts  4.82 us
    ppermute x6, waiting for transfers between devices, swap_cores(): lax.ppermute(value, 'con', [(i, i ^ 1) for i in range(2 * SIDE * SIDE)])  3.56 us
  transfers between devices with their start and end apart: 34, of which 10 were waited for; matrix products, arithmetic and copies ran while one was open for 5% of the time, Pallas kernels for 25%

profile of v4, /device:TPU:1, one launch (start us, length us, event | category | flops | bytes accessed | tf_op | source)
XLA Modules:
  0.0 140.5 jit_solution(16012308459234006469)
XLA Ops:
  10.0 9.7 %collective-permute-done.1 = bf16[2,800,256]{2,1,0:T(8,128)(2,1)S(1)} collective-permute-done((bf16[2,800,256]{2,1,0:T(8,128)(2,1)S(1)}, bf16[2,800,256]{2,1,0:T(8,128)(2,1)S(1)}, u32[]{:S(2)}, u32[]{:S(2)}) %collective-permute-start.1) | collective-permute-done | bytes 819232 | tf_op jit(solution)/shard_map/ppermute | solution.py:50
  20.1 2.7 %collective-permute-start.8 = (bf16[800,256]{1,0:T(8,128)(2,1)S(1)}, bf16[800,256]{1,0:T(8,128)(2,1)S(1)}, u32[]{:S(2)}, u32[]{:S(2)}) collective-permute-start(bf16[800,256]{1,0:T(8,128)(2,1)S(1)} %get-tuple-element.89), channel_id=1, source_target_pairs={{0,6},{1,25},{2,0},{3,27},{4,2},{5,29},{6,4},{7,31},{8,14},{9,1},{... | collective-permute-start | bytes 1228808 | tf_op jit(solution)/shard_map/ppermute | solution.py:50
  23.0 5.1 %collective-permute-done.3 = bf16[800,256]{1,0:T(8,128)(2,1)S(1)} collective-permute-done((bf16[800,256]{1,0:T(8,128)(2,1)S(1)}, bf16[800,256]{1,0:T(8,128)(2,1)S(1)}, u32[]{:S(2)}, u32[]{:S(2)}) %collective-permute-start.3) | collective-permute-done | bytes 409632 | tf_op jit(solution)/shard_map/ppermute | solution.py:50
  29.7 2.1 %collective-permute-start.5 = (bf16[4,448,256]{2,1,0:T(8,128)(2,1)S(1)}, bf16[4,448,256]{2,1,0:T(8,128)(2,1)}, u32[]{:S(2)}, u32[]{:S(2)}) collective-permute-start(bf16[4,448,256]{2,1,0:T(8,128)(2,1)S(1)} %bitcast.34), channel_id=1, source_target_pairs={{0,24},{1,7},{2,26},{3,1},{4,28},{5,3},{6,30},{7,5},{8,0},{9,15},{... | collective-permute-start | bytes 2752520 | tf_op jit(solution)/shard_map/ppermute | solution.py:50
  35.4 7.5 %collective-permute-done.4.t1 = bf16[4,448,256]{2,1,0:T(8,128)(2,1)} collective-permute-done((bf16[4,448,256]{2,1,0:T(8,128)(2,1)S(1)}, bf16[4,448,256]{2,1,0:T(8,128)(2,1)}, u32[]{:S(2)}, u32[]{:S(2)}) %collective-permute-start.4) | collective-permute-done | bytes 917536 | tf_op jit(solution)/shard_map/ppermute | solution.py:50
  43.0 9.2 %collective-permute-done.10.t2 = bf16[4,448,256]{2,1,0:T(8,128)(2,1)} collective-permute-done((bf16[4,448,256]{2,1,0:T(8,128)(2,1)S(1)}, bf16[4,448,256]{2,1,0:T(8,128)(2,1)}, u32[]{:S(2)}, u32[]{:S(2)}) %collective-permute-start.10) | collective-permute-done | bytes 917536 | tf_op jit(solution)/shard_map/ppermute | solution.py:50
  52.1 3.2 %collective-permute-start.11 = (bf16[4,448,256]{2,1,0:T(8,128)(2,1)}, bf16[4,448,256]{2,1,0:T(8,128)(2,1)S(1)}, u32[]{:S(2)}, u32[]{:S(2)}) collective-permute-start(bf16[4,448,256]{2,1,0:T(8,128)(2,1)} %collective-permute-done.10.t2), channel_id=1, source_target_pairs={{0,24},{1,7},{2,26},{3,1},{4,28},{5,3},{6,30},{7,5},{8,0},{9,15},{... | collective-permute-start | bytes 2752520 | tf_op jit(solution)/shard_map/ppermute | solution.py:50
  57.8 2.7 %collective-permute-start.16 = (bf16[4,352,256]{2,1,0:T(8,128)(2,1)S(1)}, bf16[4,352,256]{2,1,0:T(8,128)(2,1)}, u32[]{:S(2)}, u32[]{:S(2)}) collective-permute-start(bf16[4,352,256]{2,1,0:T(8,128)(2,1)S(1)} %bitcast.39), channel_id=1, source_target_pairs={{0,24},{1,7},{2,26},{3,1},{4,28},{5,3},{6,30},{7,5},{8,0},{9,15},{... | collective-permute-start | bytes 2162696 | tf_op jit(solution)/shard_map/ppermute | solution.py:50
  60.6 1.9 %collective-permute-done.6.t3 = bf16[4,448,256]{2,1,0:T(8,128)(2,1)S(1)} collective-permute-done((bf16[4,448,256]{2,1,0:T(8,128)(2,1)}, bf16[4,448,256]{2,1,0:T(8,128)(2,1)S(1)}, u32[]{:S(2)}, u32[]{:S(2)}) %collective-permute-start.6) | collective-permute-done | bytes 917536 | tf_op jit(solution)/shard_map/ppermute | solution.py:50
  62.5 2.7 %collective-permute-start.13 = (bf16[4,352,256]{2,1,0:T(8,128)(2,1)S(1)}, bf16[4,352,256]{2,1,0:T(8,128)(2,1)}, u32[]{:S(2)}, u32[]{:S(2)}) collective-permute-start(bf16[4,352,256]{2,1,0:T(8,128)(2,1)S(1)} %bitcast.43), channel_id=1, source_target_pairs={{0,24},{1,7},{2,26},{3,1},{4,28},{5,3},{6,30},{7,5},{8,0},{9,15},{... | collective-permute-start | bytes 2162696 | tf_op jit(solution)/shard_map/ppermute | solution.py:50
  65.1 8.9 %shard_map.91 = (f32[2,112,512]{2,1,0:T(8,128)S(1)}, s16[2,112,512]{2,1,0:T(8,128)(2,1)S(1)}, s16[2,112,512]{2,1,0:T(8,128)(2,1)S(1)}, s16[2,112,512]{2,1,0:T(8,128)(2,1)S(1)}) custom-call(s32[21]{0:T(128)S(1)} %pad_add_fusion.table, bf16[4,448,256]{2,1,0:T(8,128)(2,1)S(1)} %bitcast.35, bf16[4,448,256]{2,1,0:T(8,128)(2,1)} %collective-permute-done.4.t1, ...), custom_call_target="tpu_custom_call" | custom-call | flops 3584000000 | bytes 24000000 | tf_op jit(solution)/shard_map/pallas_call | solution.py:130
  74.8 1.6 %collective-permute-start.17 = (s16[2,112,512]{2,1,0:T(8,128)(2,1)S(1)}, s16[2,112,512]{2,1,0:T(8,128)(2,1)S(1)}, u32[]{:S(2)}, u32[]{:S(2)}) collective-permute-start(s16[2,112,512]{2,1,0:T(8,128)(2,1)S(1)} %get-tuple-element.53), channel_id=1, source_target_pairs={{0,32},{32,64},{64,96},{96,0},{1,33},{33,65},{65,97},{97,1},{2,34}... | collective-permute-start | bytes 688136 | tf_op jit(solution)/shard_map/ppermute | solution.py:58
  76.4 8.9 %shard_map.92 = (f32[2,112,512]{2,1,0:T(8,128)S(1)}, s16[2,112,512]{2,1,0:T(8,128)(2,1)S(1)}, s16[2,112,512]{2,1,0:T(8,128)(2,1)S(1)}, s16[2,112,512]{2,1,0:T(8,128)(2,1)S(1)}) custom-call(s32[21]{0:T(128)S(1)} %pad_add_fusion.table, bf16[4,448,256]{2,1,0:T(8,128)(2,1)S(1)} %bitcast.38, bf16[4,448,256]{2,1,0:T(8,128)(2,1)} %collective-permute-done.9.t1, ...), custom_call_target="tpu_custom_call" | custom-call | flops 3584000000 | bytes 24000000 | tf_op jit(solution)/shard_map/pallas_call | solution.py:130
  88.2 2.7 %collective-permute-start.18 = (bf16[4,352,256]{2,1,0:T(8,128)(2,1)}, bf16[4,352,256]{2,1,0:T(8,128)(2,1)S(1)}, u32[]{:S(2)}, u32[]{:S(2)}) collective-permute-start(bf16[4,352,256]{2,1,0:T(8,128)(2,1)} %collective-permute-done.16.t2), channel_id=1, source_target_pairs={{0,24},{1,7},{2,26},{3,1},{4,28},{5,3},{6,30},{7,5},{8,0},{9,15},{... | collective-permute-start | bytes 2162696 | tf_op jit(solution)/shard_map/ppermute | solution.py:50
  91.7 1.7 %collective-permute-start.24 = (s16[2,112,512]{2,1,0:T(8,128)(2,1)}, s16[2,112,512]{2,1,0:T(8,128)(2,1)S(1)}, u32[]{:S(2)}, u32[]{:S(2)}) collective-permute-start(s16[2,112,512]{2,1,0:T(8,128)(2,1)} %copy-done.9), channel_id=1, source_target_pairs={{0,32},{32,64},{64,96},{96,0},{1,33},{33,65},{65,97},{97,1},{2,34}... | collective-permute-start | bytes 688136 | tf_op jit(solution)/shard_map/ppermute | solution.py:58
  93.4 1.8 %collective-permute-start.19 = (s16[2,112,512]{2,1,0:T(8,128)(2,1)}, s16[2,112,512]{2,1,0:T(8,128)(2,1)S(1)}, u32[]{:S(2)}, u32[]{:S(2)}) collective-permute-start(s16[2,112,512]{2,1,0:T(8,128)(2,1)} %copy-done.8), channel_id=1, source_target_pairs={{0,64},{32,96},{64,0},{96,32},{1,65},{33,97},{65,1},{97,33},{2,66}... | collective-permute-start | bytes 688136 | tf_op jit(solution)/shard_map/ppermute | solution.py:58
  95.1 2.0 %collective-permute-start.20 = (s16[2,112,512]{2,1,0:T(8,128)(2,1)S(1)}, s16[2,112,512]{2,1,0:T(8,128)(2,1)S(1)}, u32[]{:S(2)}, u32[]{:S(2)}) collective-permute-start(s16[2,112,512]{2,1,0:T(8,128)(2,1)S(1)} %get-tuple-element.58), channel_id=1, source_target_pairs={{0,96},{32,0},{64,32},{96,64},{1,97},{33,1},{65,33},{97,65},{2,98}... | collective-permute-start | bytes 688136 | tf_op jit(solution)/shard_map/ppermute | solution.py:58
  97.1 8.3 %shard_map.93 = (f32[2,88,512]{2,1,0:T(8,128)S(1)}, s16[2,88,512]{2,1,0:T(8,128)(2,1)S(1)}, s16[2,88,512]{2,1,0:T(8,128)(2,1)S(1)}, s16[2,88,512]{2,1,0:T(8,128)(2,1)S(1)}) custom-call(s32[21]{0:T(128)S(1)} %pad_add_fusion.table, bf16[4,352,256]{2,1,0:T(8,128)(2,1)S(1)} %bitcast.44, bf16[4,352,256]{2,1,0:T(8,128)(2,1)} %collective-permute-done.12.t1, ...), custom_call_target="tpu_custom_call" | custom-call | flops 2816000000 | bytes 24000000 | tf_op jit(solution)/shard_map/pallas_call | solution.py:130
  105.5 1.9 %collective-permute-start.26 = (s16[2,112,512]{2,1,0:T(8,128)(2,1)S(1)}, s16[2,112,512]{2,1,0:T(8,128)(2,1)S(1)}, u32[]{:S(2)}, u32[]{:S(2)}) collective-permute-start(s16[2,112,512]{2,1,0:T(8,128)(2,1)S(1)} %copy-done.5), channel_id=1, source_target_pairs={{0,96},{32,0},{64,32},{96,64},{1,97},{33,1},{65,33},{97,65},{2,98}... | collective-permute-start | bytes 688136 | tf_op jit(solution)/shard_map/ppermute | solution.py:58
  107.4 2.5 %collective-permute-start.22 = (s16[2,88,512]{2,1,0:T(8,128)(2,1)S(1)}, s16[2,88,512]{2,1,0:T(8,128)(2,1)S(1)}, u32[]{:S(2)}, u32[]{:S(2)}) collective-permute-start(s16[2,88,512]{2,1,0:T(8,128)(2,1)S(1)} %get-tuple-element.62), channel_id=1, source_target_pairs={{0,64},{32,96},{64,0},{96,32},{1,65},{33,97},{65,1},{97,33},{2,66}... | collective-permute-start | bytes 540680 | tf_op jit(solution)/shard_map/ppermute | solution.py:58
  110.6 7.7 %shard_map.94 = (f32[2,88,512]{2,1,0:T(8,128)S(1)}, s16[2,88,512]{2,1,0:T(8,128)(2,1)S(1)}, s16[2,88,512]{2,1,0:T(8,128)(2,1)S(1)}, s16[2,88,512]{2,1,0:T(8,128)(2,1)S(1)}) custom-call(s32[21]{0:T(128)S(1)} %pad_add_fusion.table, bf16[4,352,256]{2,1,0:T(8,128)(2,1)S(1)} %bitcast.41, bf16[4,352,256]{2,1,0:T(8,128)(2,1)} %collective-permute-done.15.t1, ...), custom_call_target="tpu_custom_call" | custom-call | flops 2816000000 | bytes 24000000 | tf_op jit(solution)/shard_map/pallas_call | solution.py:130
  118.7 5.3 %collective-permute-start.30 = (bf16[112,500]{1,0:T(8,128)(2,1)S(1)}, bf16[112,500]{1,0:T(8,128)(2,1)S(1)}, u32[]{:S(2)}, u32[]{:S(2)}) collective-permute-start(bf16[112,500]{1,0:T(8,128)(2,1)S(1)} %get-tuple-element.75), channel_id=1, source_target_pairs={{0,1},{1,0},{2,3},{3,2},{4,5},{5,4},{6,7},{7,6},{8,9},{9,8},{10,11... | collective-permute-start | bytes 336008 | tf_op jit(solution)/shard_map/ppermute | solution.py:54
  126.1 1.8 %collective-permute-start.28 = (s16[2,88,512]{2,1,0:T(8,128)(2,1)S(1)}, s16[2,88,512]{2,1,0:T(8,128)(2,1)S(1)}, u32[]{:S(2)}, u32[]{:S(2)}) collective-permute-start(s16[2,88,512]{2,1,0:T(8,128)(2,1)S(1)} %get-tuple-element.71), channel_id=1, source_target_pairs={{0,64},{32,96},{64,0},{96,32},{1,65},{33,97},{65,1},{97,33},{2,66}... | collective-permute-start | bytes 540680 | tf_op jit(solution)/shard_map/ppermute | solution.py:58
  131.6 4.5 %collective-permute-done.28.code2 = s16[2,88,512]{2,1,0:T(8,128)(2,1)S(1)} collective-permute-done((s16[2,88,512]{2,1,0:T(8,128)(2,1)S(1)}, s16[2,88,512]{2,1,0:T(8,128)(2,1)S(1)}, u32[]{:S(2)}, u32[]{:S(2)}) %collective-permute-start.28) | collective-permute-done | bytes 180256 | tf_op jit(solution)/shard_map/ppermute | solution.py:58
  (168 shorter events, 33.7 us)
Async XLA Ops:
  5.5 56.9 %collective-permute-start.7 = (bf16[4,4000,500]{2,1,0:T(8,128)(2,1)}, bf16[4,4000,500]{2,1,0:T(8,128)(2,1)}, u32[]{:S(2)}, u32[]{:S(2)}) collective-permute-start(bf16[4,4000,500]{2,1,0:T(8,128)(2,1)} %w_own.3), channel_id=1, source_target_pairs={{0,1},{1,0},{2,3},{3,2},{4,5},{5,4},{6,7},{7,6},{8,9},{9,8},{10,11... | collective-permute-start | bytes 48000008 | tf_op jit(solution)/shard_map/ppermute | solution.py:54
  6.8 12.9 %collective-permute-start.1 = (bf16[2,800,256]{2,1,0:T(8,128)(2,1)S(1)}, bf16[2,800,256]{2,1,0:T(8,128)(2,1)S(1)}, u32[]{:S(2)}, u32[]{:S(2)}) collective-permute-start(bf16[2,800,256]{2,1,0:T(8,128)(2,1)S(1)} %pad.4), channel_id=1, source_target_pairs={{0,2},{1,9},{2,4},{3,11},{4,6},{5,13},{6,0},{7,15},{8,10},{9,17},{... | collective-permute-start | bytes 2457608 | tf_op jit(solution)/shard_map/ppermute | solution.py:50
  8.4 11.7 %collective-permute-start.2 = (bf16[2,800,256]{2,1,0:T(8,128)(2,1)S(1)}, bf16[2,800,256]{2,1,0:T(8,128)(2,1)S(1)}, u32[]{:S(2)}, u32[]{:S(2)}) collective-permute-start(bf16[2,800,256]{2,1,0:T(8,128)(2,1)S(1)} %pad.4), channel_id=1, source_target_pairs={{0,6},{1,25},{2,0},{3,27},{4,2},{5,29},{6,4},{7,31},{8,14},{9,1},{... | collective-permute-start | bytes 2457608 | tf_op jit(solution)/shard_map/ppermute | solution.py:50
  29.0 13.9 %collective-permute-start.4 = (bf16[4,448,256]{2,1,0:T(8,128)(2,1)S(1)}, bf16[4,448,256]{2,1,0:T(8,128)(2,1)}, u32[]{:S(2)}, u32[]{:S(2)}) collective-permute-start(bf16[4,448,256]{2,1,0:T(8,128)(2,1)S(1)} %bitcast.33), channel_id=1, source_target_pairs={{0,8},{1,3},{2,10},{3,5},{4,12},{5,7},{6,14},{7,1},{8,16},{9,11},{... | collective-permute-start | bytes 2752520 | tf_op jit(solution)/shard_map/ppermute | solution.py:50
  29.7 26.8 %collective-permute-start.5 = (bf16[4,448,256]{2,1,0:T(8,128)(2,1)S(1)}, bf16[4,448,256]{2,1,0:T(8,128)(2,1)}, u32[]{:S(2)}, u32[]{:S(2)}) collective-permute-start(bf16[4,448,256]{2,1,0:T(8,128)(2,1)S(1)} %bitcast.34), channel_id=1, source_target_pairs={{0,24},{1,7},{2,26},{3,1},{4,28},{5,3},{6,30},{7,5},{8,0},{9,15},{... | collective-permute-start | bytes 2752520 | tf_op jit(solution)/shard_map/ppermute | solution.py:50
  32.6 19.6 %collective-permute-start.10 = (bf16[4,448,256]{2,1,0:T(8,128)(2,1)S(1)}, bf16[4,448,256]{2,1,0:T(8,128)(2,1)}, u32[]{:S(2)}, u32[]{:S(2)}) collective-permute-start(bf16[4,448,256]{2,1,0:T(8,128)(2,1)S(1)} %bitcast.36), channel_id=1, source_target_pairs={{0,24},{1,7},{2,26},{3,1},{4,28},{5,3},{6,30},{7,5},{8,0},{9,15},{... | collective-permute-start | bytes 2752520 | tf_op jit(solution)/shard_map/ppermute | solution.py:50
  34.9 22.8 %collective-permute-start.9 = (bf16[4,448,256]{2,1,0:T(8,128)(2,1)S(1)}, bf16[4,448,256]{2,1,0:T(8,128)(2,1)}, u32[]{:S(2)}, u32[]{:S(2)}) collective-permute-start(bf16[4,448,256]{2,1,0:T(8,128)(2,1)S(1)} %bitcast.37), channel_id=1, source_target_pairs={{0,8},{1,3},{2,10},{3,5},{4,12},{5,7},{6,14},{7,1},{8,16},{9,11},{... | collective-permute-start | bytes 2752520 | tf_op jit(solution)/shard_map/ppermute | solution.py:50
  42.9 19.6 %collective-permute-start.6 = (bf16[4,448,256]{2,1,0:T(8,128)(2,1)}, bf16[4,448,256]{2,1,0:T(8,128)(2,1)S(1)}, u32[]{:S(2)}, u32[]{:S(2)}) collective-permute-start(bf16[4,448,256]{2,1,0:T(8,128)(2,1)} %collective-permute-done.4.t1), channel_id=1, source_target_pairs={{0,8},{1,3},{2,10},{3,5},{4,12},{5,7},{6,14},{7,1},{8,16},{9,11},{... | collective-permute-start | bytes 2752520 | tf_op jit(solution)/shard_map/ppermute | solution.py:50
  52.1 24.3 %collective-permute-start.11 = (bf16[4,448,256]{2,1,0:T(8,128)(2,1)}, bf16[4,448,256]{2,1,0:T(8,128)(2,1)S(1)}, u32[]{:S(2)}, u32[]{:S(2)}) collective-permute-start(bf16[4,448,256]{2,1,0:T(8,128)(2,1)} %collective-permute-done.10.t2), channel_id=1, source_target_pairs={{0,24},{1,7},{2,26},{3,1},{4,28},{5,3},{6,30},{7,5},{8,0},{9,15},{... | collective-permute-start | bytes 2752520 | tf_op jit(solution)/shard_map/ppermute | solution.py:50
  56.5 18.3 %collective-permute-start.12 = (bf16[4,352,256]{2,1,0:T(8,128)(2,1)S(1)}, bf16[4,352,256]{2,1,0:T(8,128)(2,1)}, u32[]{:S(2)}, u32[]{:S(2)}) collective-permute-start(bf16[4,352,256]{2,1,0:T(8,128)(2,1)S(1)} %bitcast.42), channel_id=1, source_target_pairs={{0,8},{1,3},{2,10},{3,5},{4,12},{5,7},{6,14},{7,1},{8,16},{9,11},{... | collective-permute-start | bytes 2162696 | tf_op jit(solution)/shard_map/ppermute | solution.py:50
  57.8 30.4 %collective-permute-start.16 = (bf16[4,352,256]{2,1,0:T(8,128)(2,1)S(1)}, bf16[4,352,256]{2,1,0:T(8,128)(2,1)}, u32[]{:S(2)}, u32[]{:S(2)}) collective-permute-start(bf16[4,352,256]{2,1,0:T(8,128)(2,1)S(1)} %bitcast.39), channel_id=1, source_target_pairs={{0,24},{1,7},{2,26},{3,1},{4,28},{5,3},{6,30},{7,5},{8,0},{9,15},{... | collective-permute-start | bytes 2162696 | tf_op jit(solution)/shard_map/ppermute | solution.py:50
  62.5 42.9 %collective-permute-start.15 = (bf16[4,352,256]{2,1,0:T(8,128)(2,1)S(1)}, bf16[4,352,256]{2,1,0:T(8,128)(2,1)}, u32[]{:S(2)}, u32[]{:S(2)}) collective-permute-start(bf16[4,352,256]{2,1,0:T(8,128)(2,1)S(1)} %bitcast.40), channel_id=1, source_target_pairs={{0,8},{1,3},{2,10},{3,5},{4,12},{5,7},{6,14},{7,1},{8,16},{9,11},{... | collective-permute-start | bytes 2162696 | tf_op jit(solution)/shard_map/ppermute | solution.py:50
  62.5 30.9 %collective-permute-start.13 = (bf16[4,352,256]{2,1,0:T(8,128)(2,1)S(1)}, bf16[4,352,256]{2,1,0:T(8,128)(2,1)}, u32[]{:S(2)}, u32[]{:S(2)}) collective-permute-start(bf16[4,352,256]{2,1,0:T(8,128)(2,1)S(1)} %bitcast.43), channel_id=1, source_target_pairs={{0,24},{1,7},{2,26},{3,1},{4,28},{5,3},{6,30},{7,5},{8,0},{9,15},{... | collective-permute-start | bytes 2162696 | tf_op jit(solution)/shard_map/ppermute | solution.py:50
  74.8 13.4 %collective-permute-start.17 = (s16[2,112,512]{2,1,0:T(8,128)(2,1)S(1)}, s16[2,112,512]{2,1,0:T(8,128)(2,1)S(1)}, u32[]{:S(2)}, u32[]{:S(2)}) collective-permute-start(s16[2,112,512]{2,1,0:T(8,128)(2,1)S(1)} %get-tuple-element.53), channel_id=1, source_target_pairs={{0,32},{32,64},{64,96},{96,0},{1,33},{33,65},{65,97},{97,1},{2,34}... | collective-permute-start | bytes 688136 | tf_op jit(solution)/shard_map/ppermute | solution.py:58
  76.4 18.7 %collective-permute-start.14 = (bf16[4,352,256]{2,1,0:T(8,128)(2,1)}, bf16[4,352,256]{2,1,0:T(8,128)(2,1)}, u32[]{:S(2)}, u32[]{:S(2)}) collective-permute-start(bf16[4,352,256]{2,1,0:T(8,128)(2,1)} %collective-permute-done.12.t1), channel_id=1, source_target_pairs={{0,8},{1,3},{2,10},{3,5},{4,12},{5,7},{6,14},{7,1},{8,16},{9,11},{... | collective-permute-start | bytes 2162696 | tf_op jit(solution)/shard_map/ppermute | solution.py:50
  88.2 21.8 %collective-permute-start.18 = (bf16[4,352,256]{2,1,0:T(8,128)(2,1)}, bf16[4,352,256]{2,1,0:T(8,128)(2,1)S(1)}, u32[]{:S(2)}, u32[]{:S(2)}) collective-permute-start(bf16[4,352,256]{2,1,0:T(8,128)(2,1)} %collective-permute-done.16.t2), channel_id=1, source_target_pairs={{0,24},{1,7},{2,26},{3,1},{4,28},{5,3},{6,30},{7,5},{8,0},{9,15},{... | collective-permute-start | bytes 2162696 | tf_op jit(solution)/shard_map/ppermute | solution.py:50
  91.7 13.9 %collective-permute-start.24 = (s16[2,112,512]{2,1,0:T(8,128)(2,1)}, s16[2,112,512]{2,1,0:T(8,128)(2,1)S(1)}, u32[]{:S(2)}, u32[]{:S(2)}) collective-permute-start(s16[2,112,512]{2,1,0:T(8,128)(2,1)} %copy-done.9), channel_id=1, source_target_pairs={{0,32},{32,64},{64,96},{96,0},{1,33},{33,65},{65,97},{97,1},{2,34}... | collective-permute-start | bytes 688136 | tf_op jit(solution)/shard_map/ppermute | solution.py:58
  93.4 14.0 %collective-permute-start.19 = (s16[2,112,512]{2,1,0:T(8,128)(2,1)}, s16[2,112,512]{2,1,0:T(8,128)(2,1)S(1)}, u32[]{:S(2)}, u32[]{:S(2)}) collective-permute-start(s16[2,112,512]{2,1,0:T(8,128)(2,1)} %copy-done.8), channel_id=1, source_target_pairs={{0,64},{32,96},{64,0},{96,32},{1,65},{33,97},{65,1},{97,33},{2,66}... | collective-permute-start | bytes 688136 | tf_op jit(solution)/shard_map/ppermute | solution.py:58
  95.1 12.2 %collective-permute-start.20 = (s16[2,112,512]{2,1,0:T(8,128)(2,1)S(1)}, s16[2,112,512]{2,1,0:T(8,128)(2,1)S(1)}, u32[]{:S(2)}, u32[]{:S(2)}) collective-permute-start(s16[2,112,512]{2,1,0:T(8,128)(2,1)S(1)} %get-tuple-element.58), channel_id=1, source_target_pairs={{0,96},{32,0},{64,32},{96,64},{1,97},{33,1},{65,33},{97,65},{2,98}... | collective-permute-start | bytes 688136 | tf_op jit(solution)/shard_map/ppermute | solution.py:58
  105.4 13.3 %collective-permute-start.25 = (s16[2,112,512]{2,1,0:T(8,128)(2,1)S(1)}, s16[2,112,512]{2,1,0:T(8,128)(2,1)S(1)}, u32[]{:S(2)}, u32[]{:S(2)}) collective-permute-start(s16[2,112,512]{2,1,0:T(8,128)(2,1)S(1)} %copy-done.7), channel_id=1, source_target_pairs={{0,64},{32,96},{64,0},{96,32},{1,65},{33,97},{65,1},{97,33},{2,66}... | collective-permute-start | bytes 688136 | tf_op jit(solution)/shard_map/ppermute | solution.py:58
  105.5 18.6 %collective-permute-start.26 = (s16[2,112,512]{2,1,0:T(8,128)(2,1)S(1)}, s16[2,112,512]{2,1,0:T(8,128)(2,1)S(1)}, u32[]{:S(2)}, u32[]{:S(2)}) collective-permute-start(s16[2,112,512]{2,1,0:T(8,128)(2,1)S(1)} %copy-done.5), channel_id=1, source_target_pairs={{0,96},{32,0},{64,32},{96,64},{1,97},{33,1},{65,33},{97,65},{2,98}... | collective-permute-start | bytes 688136 | tf_op jit(solution)/shard_map/ppermute | solution.py:58
  107.4 17.2 %collective-permute-start.21 = (s16[2,88,512]{2,1,0:T(8,128)(2,1)S(1)}, s16[2,88,512]{2,1,0:T(8,128)(2,1)S(1)}, u32[]{:S(2)}, u32[]{:S(2)}) collective-permute-start(s16[2,88,512]{2,1,0:T(8,128)(2,1)S(1)} %get-tuple-element.61), channel_id=1, source_target_pairs={{0,32},{32,64},{64,96},{96,0},{1,33},{33,65},{65,97},{97,1},{2,34}... | collective-permute-start | bytes 540680 | tf_op jit(solution)/shard_map/ppermute | solution.py:58
  107.4 18.7 %collective-permute-start.22 = (s16[2,88,512]{2,1,0:T(8,128)(2,1)S(1)}, s16[2,88,512]{2,1,0:T(8,128)(2,1)S(1)}, u32[]{:S(2)}, u32[]{:S(2)}) collective-permute-start(s16[2,88,512]{2,1,0:T(8,128)(2,1)S(1)} %get-tuple-element.62), channel_id=1, source_target_pairs={{0,64},{32,96},{64,0},{96,32},{1,65},{33,97},{65,1},{97,33},{2,66}... | collective-permute-start | bytes 540680 | tf_op jit(solution)/shard_map/ppermute | solution.py:58
  109.9 18.0 %collective-permute-start.23 = (s16[2,88,512]{2,1,0:T(8,128)(2,1)S(1)}, s16[2,88,512]{2,1,0:T(8,128)(2,1)S(1)}, u32[]{:S(2)}, u32[]{:S(2)}) collective-permute-start(s16[2,88,512]{2,1,0:T(8,128)(2,1)S(1)} %get-tuple-element.63), channel_id=1, source_target_pairs={{0,96},{32,0},{64,32},{96,64},{1,97},{33,1},{65,33},{97,65},{2,98}... | collective-permute-start | bytes 540680 | tf_op jit(solution)/shard_map/ppermute | solution.py:58
  (35 other events, 242.3 us)
